TPU v7x, 256 devices: a whole 4x4x8 slice. The times are simulated.
256 devices in a mesh: ctx: 64 (over x, z, core), head: 4 (over y).
Axes of the slice: x: 4, y: 4, z: 8, core: 2. Of those that a mesh axis runs over, the one named last changes fastest.
Arguments:
- queries: bfloat16 [12288, 1024], P(('ctx', 'head')), may hold values from -1.5 to 1.5, as said below
- key_inputs: bfloat16 [12288, 1024], P(('ctx', 'head')), may hold values from -1.5 to 1.5, as said below
- value_inputs: bfloat16 [12288, 1024], P(('ctx', 'head')), may hold values from -6 to 6
- out_grad: bfloat16 [12288, 1024], P(('ctx', 'head')), may hold values from -6 to 6
- attn_output: bfloat16 [12288, 1024], P(('ctx', 'head')), may hold values from -6 to 6
- gate_logits: bfloat16 [12288, 8], P(('ctx', 'head')), may hold values from 0 to 16
- lse: float32 [12288, 8], P(('ctx', 'head')), as said below
Outputs:
- query_grad: bfloat16 [12288, 1024], P(('ctx', 'head'))
- key_grad: bfloat16 [12288, 1024], P(('ctx', 'head'))
- value_grad: bfloat16 [12288, 1024], P(('ctx', 'head'))
- gate_grad: bfloat16 [12288, 8], P(('ctx', 'head'))
Inputs may be any that keep to these rules, and one draw needn't show every extreme that they name: `queries`: queries of every token. `key_inputs`: keys of every token. `lse`: the forward pass's log-sum-exp of each query's scores.
All inputs are finite; a program needn't handle non-finite values.
Results may differ from a plain program's by a relative error of at most 0.0052.
Values may be sent and summed in bfloat16 or wider, within the bound.
A program may use at most 128 MiB of HBM per device.

v0:
```python
import math

import jax
import jax.numpy as jnp
from jax import lax
from jax.sharding import PartitionSpec as P


def prefix(value, axis, combine, identity, reverse):
    devices, here = (lax.axis_size(axis), lax.axis_index(axis))
    everything = lax.all_gather(value, axis)
    start = jnp.broadcast_to(jnp.asarray(identity, value.dtype), value.shape)

    def step(k, before):
        at = devices - 1 - k if reverse else k
        reached = at > here if reverse else at < here
        new = combine(before, everything[at])
        return jnp.where(reached, new, before)

    return lax.fori_loop(0, devices, step, start)


def block_scores(query_blk, key_blk, query_curve, key_curve, query_pos, key_pos, score_scale):
    product = jnp.einsum("qhd,khd->hqk", query_blk, key_blk, preferred_element_type=jnp.float32)
    scores = score_scale * product + query_curve.T[:, :, None] - key_curve.T[:, None, :]
    causal = key_pos[None, :] <= query_pos[:, None]
    return (scores, causal)


def attention_terms(
    query_blk,
    grad_blk,
    query_curve,
    query_lse,
    query_delta,
    query_pos,
    key_blk,
    value_blk,
    key_curve,
    key_pos,
    score_scale,
):
    scores, causal = block_scores(
        query_blk, key_blk, query_curve, key_curve, query_pos, key_pos, score_scale
    )
    probs = jnp.where(causal[None], jnp.exp(scores - query_lse[:, :, None]), 0.0)
    grad_probs = jnp.einsum("qhd,khd->hqk", grad_blk, value_blk, preferred_element_type=jnp.float32)
    score_grad = probs * (grad_probs - query_delta[:, :, None])
    return (probs, score_grad)


def fold_blocks(block_step, carry_in, pieces, useful):
    piece_len = pieces[0].shape[0]
    block_len = math.gcd(piece_len, 512)

    def one_turn(turn_index, carry_now):
        offset = turn_index * block_len
        sliced = tuple(
            (lax.dynamic_slice_in_dim(member, offset, block_len, 0) for member in pieces)
        )
        return lax.cond(
            useful(offset, block_len),
            lambda carry_arg: block_step(carry_arg, sliced, offset),
            lambda carry_arg: carry_arg,
            carry_now,
        )

    return lax.fori_loop(0, piece_len // block_len, one_turn, carry_in)


def per_device(queries, key_inputs, value_inputs, out_grad, attn_output, gate_logits, lse):
    my_query, my_keys, my_values, my_grad, my_output = (
        lax.all_to_all(queries, "head", split_axis=1, concat_axis=0, tiled=True),
        lax.all_to_all(key_inputs, "head", split_axis=1, concat_axis=0, tiled=True),
        lax.all_to_all(value_inputs, "head", split_axis=1, concat_axis=0, tiled=True),
        lax.all_to_all(out_grad, "head", split_axis=1, concat_axis=0, tiled=True),
        lax.all_to_all(attn_output, "head", split_axis=1, concat_axis=0, tiled=True),
    )
    gate_float, my_lse = (
        lax.all_to_all(
            gate_logits.astype(jnp.float32), "head", split_axis=1, concat_axis=0, tiled=True
        ),
        lax.all_to_all(lse, "head", split_axis=1, concat_axis=0, tiled=True),
    )
    row_count = my_query.shape[0]
    head_count = gate_float.shape[1]
    head_width = my_query.shape[1] // head_count
    score_scale = head_width ** (-0.5)
    dev_index = lax.axis_index("ctx")
    my_start = dev_index * row_count
    my_last = my_start + row_count - 1
    query_pos = my_start + jnp.arange(row_count, dtype=jnp.int32)
    query_three = my_query.reshape(row_count, head_count, head_width)
    key_three = my_keys.reshape(row_count, head_count, head_width)
    value_three = my_values.reshape(row_count, head_count, head_width)
    grad_three = my_grad.reshape(row_count, head_count, head_width)
    output_three = my_output.reshape(row_count, head_count, head_width)
    local_curve = jnp.cumsum(jax.nn.log_sigmoid(gate_float), axis=0)
    before = prefix(local_curve[-1], "ctx", jnp.add, jnp.zeros((head_count,), jnp.float32), False)
    source = local_curve + before[None, :]
    gathered = lax.all_gather(source, "ctx", axis=0, tiled=True)
    my_curve = lax.dynamic_slice_in_dim(gathered, my_start, row_count, 0)

    def keys_useful(start_row, block_len):
        return start_row <= my_last

    def queries_useful(start_row, block_len):
        return start_row + block_len - 1 >= my_start

    zero_stat = jnp.zeros((head_count, row_count), jnp.float32)
    zero_rows = jnp.zeros((row_count, head_count, head_width), jnp.float32)
    log_total = my_lse.T
    row_delta = jnp.sum(grad_three.astype(jnp.float32) * output_three.astype(jnp.float32), axis=2).T

    def add_query_side(carry_now, sliced, start_row):
        query_acc, row_acc = carry_now
        key_blk = sliced[0].reshape(-1, head_count, head_width)
        value_blk = sliced[1].reshape(-1, head_count, head_width)
        block_len = key_blk.shape[0]
        key_curve = lax.dynamic_slice_in_dim(gathered, start_row, block_len, 0)
        key_pos = start_row + jnp.arange(block_len, dtype=jnp.int32)
        probs, score_grad = attention_terms(
            query_three,
            grad_three,
            my_curve,
            log_total,
            row_delta,
            query_pos,
            key_blk,
            value_blk,
            key_curve,
            key_pos,
            score_scale,
        )
        query_acc = query_acc + jnp.einsum(
            "hqk,khd->qhd",
            score_grad.astype(jnp.bfloat16),
            key_blk,
            preferred_element_type=jnp.float32,
        )
        return (query_acc, row_acc + jnp.sum(score_grad, axis=2))

    query_acc, row_acc = fold_blocks(
        add_query_side,
        (zero_rows, zero_stat),
        (
            lax.all_gather(my_keys, "ctx", axis=0, tiled=True),
            lax.all_gather(my_values, "ctx", axis=0, tiled=True),
        ),
        keys_useful,
    )
    all_lse, all_delta = (
        lax.all_gather(my_lse, "ctx", axis=0, tiled=True),
        lax.all_gather(row_delta.T, "ctx", axis=0, tiled=True),
    )

    def add_key_side(carry_now, sliced, start_row):
        key_acc, value_acc, column_acc = carry_now
        query_blk = sliced[0].reshape(-1, head_count, head_width)
        grad_blk = sliced[1].reshape(-1, head_count, head_width)
        block_len = query_blk.shape[0]
        query_curve = lax.dynamic_slice_in_dim(gathered, start_row, block_len, 0)
        query_lse = lax.dynamic_slice_in_dim(all_lse, start_row, block_len, 0).T
        query_delta = lax.dynamic_slice_in_dim(all_delta, start_row, block_len, 0).T
        other_pos = start_row + jnp.arange(block_len, dtype=jnp.int32)
        probs, score_grad = attention_terms(
            query_blk,
            grad_blk,
            query_curve,
            query_lse,
            query_delta,
            other_pos,
            key_three,
            value_three,
            my_curve,
            query_pos,
            score_scale,
        )
        value_acc = value_acc + jnp.einsum(
            "hqk,qhd->khd", probs.astype(jnp.bfloat16), grad_blk, preferred_element_type=jnp.float32
        )
        key_acc = key_acc + jnp.einsum(
            "hqk,qhd->khd",
            score_grad.astype(jnp.bfloat16),
            query_blk,
            preferred_element_type=jnp.float32,
        )
        return (key_acc, value_acc, column_acc + jnp.sum(score_grad, axis=1))

    key_acc, value_acc, column_acc = fold_blocks(
        add_key_side,
        (zero_rows, zero_rows, zero_stat),
        (
            lax.all_gather(my_query, "ctx", axis=0, tiled=True),
            lax.all_gather(my_grad, "ctx", axis=0, tiled=True),
        ),
        queries_useful,
    )
    curve_grad = row_acc - column_acc
    local_rev = jnp.flip(jnp.cumsum(jnp.flip(curve_grad, 1), axis=1), 1)
    shard_total = jnp.sum(curve_grad, axis=1)
    after = prefix(shard_total, "ctx", jnp.add, jnp.zeros((head_count,), jnp.float32), True)
    gate_sum = local_rev + after[:, None]
    gate_grad = (gate_sum.T * jax.nn.sigmoid(-gate_float)).astype(jnp.bfloat16)
    query_grad = (
        (score_scale * query_acc).reshape(row_count, head_count * head_width).astype(jnp.bfloat16)
    )
    key_grad = (
        (score_scale * key_acc).reshape(row_count, head_count * head_width).astype(jnp.bfloat16)
    )
    value_grad = value_acc.reshape(row_count, head_count * head_width).astype(jnp.bfloat16)
    return (
        lax.all_to_all(query_grad, "head", split_axis=0, concat_axis=1, tiled=True),
        lax.all_to_all(key_grad, "head", split_axis=0, concat_axis=1, tiled=True),
        lax.all_to_all(value_grad, "head", split_axis=0, concat_axis=1, tiled=True),
        lax.all_to_all(gate_grad, "head", split_axis=0, concat_axis=1, tiled=True),
    )


def solution(mesh):
    placed = (
        P(("ctx", "head"), None),
        P(("ctx", "head"), None),
        P(("ctx", "head"), None),
        P(("ctx", "head"), None),
        P(("ctx", "head"), None),
        P(("ctx", "head"), None),
        P(("ctx", "head"), None),
    )
    return jax.shard_map(
        per_device,
        mesh=mesh,
        in_specs=placed,
        out_specs=(
            P(("ctx", "head"), None),
            P(("ctx", "head"), None),
            P(("ctx", "head"), None),
            P(("ctx", "head"), None),
        ),
        check_vma=False,
    )
```

profile of v0, /device:TPU:1, one launch (start us, length us, event | category | flops | bytes accessed | tf_op | source)
XLA Modules:
  0.0 585.0 jit_solution(9104188152661813660)
XLA Ops:
  8.1 9.6 %all_to_all.192 = bf16[48,4,256]{2,0,1:T(8,128)(2,1)} all-to-all(bf16[48,4,256]{2,0,1:T(8,128)(2,1)S(1)} %bitcast.177), channel_id=1, replica_groups=mesh['ctx'=64,'head'=4] {'head'}, dimensions={1} | all-to-all | bytes 196608 | tf_op jit(solution)/shard_map/all_to_all | solution.py:74
  18.6 7.7 %all_to_all.193 = bf16[48,4,256]{2,0,1:T(8,128)(2,1)} all-to-all(bf16[48,4,256]{2,0,1:T(8,128)(2,1)S(1)} %bitcast.178), channel_id=1, replica_groups=mesh['ctx'=64,'head'=4] {'head'}, dimensions={1} | all-to-all | bytes 196608 | tf_op jit(solution)/shard_map/all_to_all | solution.py:75
  27.3 7.7 %all_to_all.194 = bf16[48,4,256]{2,0,1:T(8,128)(2,1)} all-to-all(bf16[48,4,256]{2,0,1:T(8,128)(2,1)S(1)} %bitcast.179), channel_id=1, replica_groups=mesh['ctx'=64,'head'=4] {'head'}, dimensions={1} | all-to-all | bytes 196608 | tf_op jit(solution)/shard_map/all_to_all | solution.py:73
  35.0 3.3 all-to-all-start.3
  38.3 1.3 convert.3
  39.6 2.8 all-to-all-done.3
  42.4 3.2 all-to-all-start.2
  45.7 1.5 copy.256
  47.2 1.5 copy.255
  48.7 1.3 dynamic-slice
  50.8 4.2 all-to-all-start.5
  56.4 48.6 %all-gather.1 = f32[64,1,2]{2,1,0:T(1,128)S(1)} all-gather(f32[1,1,2]{2,1,0:T(1,128)S(1)} %bitcast.202), channel_id=1, replica_groups=mesh['ctx'=64,'head'=4] {'ctx'}, dimensions={0}, use_global_device_ids=true | all-gather | bytes 520 | tf_op jit(solution)/shard_map/all_gather | solution.py:11
  105.0 4.5 all-to-all-start.6
  110.1 2.6 while.70
  112.8 47.9 %all-gather.2 = f32[64,192,2]{1,2,0:T(2,128)S(1)} all-gather(f32[1,192,2]{1,2,0:T(2,128)S(1)} %fusion.26), channel_id=1, replica_groups=mesh['ctx'=64,'head'=4] {'ctx'}, dimensions={0}, use_global_device_ids=true | all-gather | bytes 99840 | tf_op jit(solution)/shard_map/all_gather | solution.py:101
  160.9 48.3 %all-gather.3 = f32[64,192,2]{1,2,0:T(2,128)S(1)} all-gather(f32[1,192,2]{1,2,0:T(2,128)S(1)} %reshape.213), channel_id=1, replica_groups=mesh['ctx'=64,'head'=4] {'ctx'}, dimensions={0}, use_global_device_ids=true | all-gather | bytes 99840 | tf_op jit(solution)/shard_map/all_gather | solution.py:153
  211.9 47.7 %all-gather.4 = f32[64,192,2]{1,2,0:T(2,128)S(1)} all-gather(f32[1,192,2]{1,2,0:T(2,128)S(1)} %copy.218), channel_id=1, replica_groups=mesh['ctx'=64,'head'=4] {'ctx'}, dimensions={0}, use_global_device_ids=true | all-gather | bytes 99840 | tf_op jit(solution)/shard_map/all_gather | solution.py:154
  260.0 8.6 %copy.209 = bf16[12288,256]{0,1:T(8,128)(2,1)} copy(bf16[12288,256]{1,0:T(8,128)(2,1)} %all-gather.10.cloned.1.call-done) | data formatting | bytes 12582912
  268.6 8.7 %copy.211 = bf16[12288,256]{0,1:T(8,128)(2,1)} copy(bf16[12288,256]{1,0:T(8,128)(2,1)} %all-gather.12.cloned.1.call-done) | data formatting | bytes 12582912
  277.3 8.7 %copy.220 = bf16[12288,256]{0,1:T(8,128)(2,1)} copy(bf16[12288,256]{1,0:T(8,128)(2,1)} %all-gather.14.cloned.1.call-done) | data formatting | bytes 12582912
  286.0 3.6 while.69
  286.0 2.3 conditional.7
  286.0 1.1 constant_dynamic-slice_fusion
  289.6 54.1 %all-gather.16.cloned.1.call-done = bf16[12288,256]{1,0:T(8,128)(2,1)} async-done(((bf16[192,256]{1,0:T(8,128)(2,1)}), bf16[12288,256]{1,0:T(8,128)(2,1)}) %all-gather.16.cloned.1.call-update) | async-done | bytes 6291472 | tf_op jit(solution)/shard_map/all_gather | solution.py:195
  343.7 8.6 %copy.222 = bf16[12288,256]{0,1:T(8,128)(2,1)} copy(bf16[12288,256]{1,0:T(8,128)(2,1)} %all-gather.16.cloned.1.call-done) | data formatting | bytes 12582912
  352.3 63.6 %while.72 = (s32[]{:T(128)}, f32[192,2,128]{2,0,1:T(8,128)S(1)}, f32[192,2,128]{2,0,1:T(8,128)S(1)}, f32[2,192]{1,0:T(2,128)S(1)}, s32[]{:T(128)}, /*index=5*/bf...) while((s32[]{:T(128)}, f32[192,2,128]{2,0,1:T(8,128)S(1)}, ...), condition=%wide.region_14.15_spmd.clone.clone, body=%wide.region_10.14_spmd.clone.clone.sunk | while | flops 203489984 | bytes 6474649 | solution.py:68
  352.4 2.6 conditional.8
  352.4 1.1 constant_dynamic-slice_fusion.2
  355.0 2.6 conditional.8
  355.0 1.1 constant_dynamic-slice_fusion.2
  357.7 2.6 conditional.8
  357.7 1.1 constant_dynamic-slice_fusion.2
  360.3 2.6 conditional.8
  360.3 1.1 constant_dynamic-slice_fusion.2
  363.0 2.6 conditional.8
  365.6 2.6 conditional.8
  368.3 2.6 conditional.8
  370.9 2.6 conditional.8
  373.6 2.6 conditional.8
  376.2 2.6 conditional.8
  378.9 2.6 conditional.8
  381.5 2.6 conditional.8
  384.2 2.6 conditional.8
  386.8 2.6 conditional.8
  389.5 2.6 conditional.8
  392.1 2.6 conditional.8
  394.8 2.6 conditional.8
  397.4 2.6 conditional.8
  400.1 2.6 conditional.8
  402.7 2.6 conditional.8
  405.3 2.6 conditional.8
  408.0 2.6 conditional.8
  410.6 2.6 conditional.8
  413.3 2.6 conditional.8
  417.7 123.6 %all-reduce.2 = f32[128]{0:T(128)S(1)} all-reduce(f32[128]{0:T(128)S(1)} %dynamic-update-slice), channel_id=2, replica_groups=mesh['ctx'=64,'head'=4] {'ctx'}, use_global_device_ids=true, to_apply=%add.2 | all-reduce | flops 128 | bytes 1024
  541.5 3.0 while.71
  545.3 4.1 all-to-all-start.10
  550.2 3.2 all-to-all-done.10
  553.4 3.3 all-to-all-start.7
  557.6 3.8 all-to-all-done.7
  561.4 3.3 all-to-all-start.8
  565.5 3.8 all-to-all-done.8
  569.3 3.3 all-to-all-start.9
  573.9 3.3 all-to-all-done.9
  (565 shorter events, 75.9 us)
Async XLA Ops:
  7.2 252.8 %all-gather.10.cloned.1.call-start = ((), (), s32[]{:S(2)}) async-start(), calls=%async_computation.11 | async-start | bytes 6389760 | tf_op jit(solution)/shard_map/all_gather | solution.py:147
  17.7 242.1 %copy-start.1 = (bf16[48,4,256]{2,0,1:T(8,128)(2,1)S(1)}, bf16[48,4,256]{2,0,1:T(8,128)(2,1)}, u32[]{:S(2)}) copy-start(bf16[48,4,256]{2,0,1:T(8,128)(2,1)} %all_to_all.192) | copy-start | bytes 294916
  17.7 250.9 %all-gather.12.cloned.1.call-start = ((), (), s32[]{:S(2)}) async-start(), calls=%async_computation.12 | async-start | bytes 6389760 | tf_op jit(solution)/shard_map/all_gather | solution.py:148
  26.3 233.5 %copy-start.2 = (bf16[48,4,256]{2,0,1:T(8,128)(2,1)S(1)}, bf16[48,4,256]{2,0,1:T(8,128)(2,1)}, u32[]{:S(2)}) copy-start(bf16[48,4,256]{2,0,1:T(8,128)(2,1)} %all_to_all.193) | copy-start | bytes 294916
  26.4 250.9 %all-gather.14.cloned.1.call-start = ((), (), s32[]{:S(2)}) async-start(), calls=%async_computation.13 | async-start | bytes 6389760 | tf_op jit(solution)/shard_map/all_gather | solution.py:194
  35.0 7.4 %all-to-all-start.3 = ((f32[48,4,2]{0,2,1:T(2,128)}), f32[48,4,2]{0,2,1:T(2,128)S(1)}, u32[]{:S(2)}, u32[]{:S(2)}) async-start(f32[48,4,2]{0,2,1:T(2,128)} %bitcast.197), calls=%async_computation.3 | async-start | bytes 8192 | tf_op jit(solution)/shard_map/all_to_all | solution.py:83
  42.4 8.4 %all-to-all-start.2 = ((f32[48,4,2]{0,2,1:T(2,128)}), f32[48,4,2]{0,2,1:T(2,128)S(1)}, u32[]{:S(2)}, u32[]{:S(2)}) async-start(f32[48,4,2]{0,2,1:T(2,128)} %convert.3), calls=%async_computation.2 | async-start | bytes 8192 | tf_op jit(solution)/shard_map/all_to_all | solution.py:80
  50.8 54.2 %all-to-all-start.5 = ((bf16[48,4,256]{2,0,1:T(8,128)(2,1)}), bf16[48,4,256]{2,0,1:T(8,128)(2,1)S(1)}, u32[]{:S(2)}, u32[]{:S(2)}) async-start(bf16[48,4,256]{2,0,1:T(8,128)(2,1)} %bitcast.143), calls=%async_computation.5 | async-start | bytes 196608 | tf_op jit(solution)/shard_map/all_to_all | solution.py:76
  105.0 4.5 copy-start
  105.0 105.4 %all-to-all-start.6 = ((bf16[48,4,256]{2,0,1:T(8,128)(2,1)}), bf16[48,4,256]{2,0,1:T(8,128)(2,1)S(1)}, u32[]{:S(2)}, u32[]{:S(2)}) async-start(bf16[48,4,256]{2,0,1:T(8,128)(2,1)} %bitcast.142), calls=%async_computation.6 | async-start | bytes 196608 | tf_op jit(solution)/shard_map/all_to_all | solution.py:77
  109.5 234.1 %all-gather.16.cloned.1.call-start = ((), (), s32[]{:S(2)}) async-start(), calls=%async_computation.14 | async-start | bytes 6389760 | tf_op jit(solution)/shard_map/all_gather | solution.py:195
  545.3 8.1 %all-to-all-start.10 = ((bf16[4,48,2]{1,2,0:T(2,128)(2,1)}), bf16[4,48,2]{1,2,0:T(2,128)(2,1)S(1)}, u32[]{:S(2)}, u32[]{:S(2)}) async-start(bf16[4,48,2]{1,2,0:T(2,128)(2,1)} %copy.229), calls=%async_computation.10 | async-start | bytes 4096 | tf_op jit(solution)/shard_map/all_to_all | solution.py:216
  553.4 7.9 %all-to-all-start.7 = ((bf16[4,48,256]{2,1,0:T(8,128)(2,1)}), bf16[4,48,256]{2,1,0:T(8,128)(2,1)S(1)}, u32[]{:S(2)}, u32[]{:S(2)}) async-start(bf16[4,48,256]{2,1,0:T(8,128)(2,1)} %convert_element_type.80), calls=%async_computation.7 | async-start | bytes 196608 | tf_op jit(solution)/shard_map/all_to_all | solution.py:213
  561.4 7.9 %all-to-all-start.8 = ((bf16[4,48,256]{2,1,0:T(8,128)(2,1)}), bf16[4,48,256]{2,1,0:T(8,128)(2,1)S(1)}, u32[]{:S(2)}, u32[]{:S(2)}) async-start(bf16[4,48,256]{2,1,0:T(8,128)(2,1)} %convert_element_type.82), calls=%async_computation.8 | async-start | bytes 196608 | tf_op jit(solution)/shard_map/all_to_all | solution.py:214
  569.3 7.9 %all-to-all-start.9 = ((bf16[4,48,256]{2,1,0:T(8,128)(2,1)}), bf16[4,48,256]{2,1,0:T(8,128)(2,1)S(1)}, u32[]{:S(2)}, u32[]{:S(2)}) async-start(bf16[4,48,256]{2,1,0:T(8,128)(2,1)} %convert_element_type.84), calls=%async_computation.9 | async-start | bytes 196608 | tf_op jit(solution)/shard_map/all_to_all | solution.py:215
Sparse Core Ops, SparseCore 0:
  17.8 83.7 all-gather.9
  104.4 77.7 all-gather.11
  185.0 77.6 all-gather.13
  265.8 77.8 all-gather.15
where the time goes:
time: 591 us; the launch traced here: 585 us
  blocking collectives  341 us (58%)
  local copies, waits for them, and re-layouts  79.2 us (13%)
  waiting for transfers between devices  71.5 us (12%)
  matrix products  31.7 us (5%)
  starting transfers between devices  29.4 us (5%)
  between operations  14.7 us (2%)
  other arithmetic  9.45 us (2%)
  loops' own time  7.85 us (1%)
    unnamed x1, blocking collectives  124 us
    all_gather x1, waiting for transfers between devices, per_device(): lax.all_gather(my_grad, 'ctx', axis=0, tiled=True)  54.1 us
    all_gather x1, blocking collectives, prefix(): everything = lax.all_gather(value, axis)  48.6 us
    all_gather x1, blocking collectives, per_device(): lax.all_gather(my_lse, 'ctx', axis=0, tiled=True)  48.3 us
    all_gather x1, blocking collectives, per_device(): gathered = lax.all_gather(source, 'ctx', axis=0, tiled=True)  47.9 us
    all_gather x1, blocking collectives, per_device(): lax.all_gather(row_delta.T, 'ctx', axis=0, tiled=True)  47.7 us
    unnamed x29, local copies, waits for them, and re-layouts  37.8 us
    dynamic_slice x25, local copies, waits for them, and re-layouts, one_turn(): lax.dynamic_slice_in_dim(member, offset, block_len, 0)  26.8 us
  transfers between devices with their start and end apart: 12, of which 6 were waited for; matrix products, arithmetic and copies ran while one was open for 8% of the time, Pallas kernels for 0%

commit v1 on v0

v1 whole, which is shorter than its diff:
```python
import functools
import math

import jax
import jax.numpy as jnp
from jax import lax
from jax.experimental import pallas as pl
from jax.experimental.pallas import tpu as pltpu
from jax.sharding import PartitionSpec as P

CORES = 2
LOG2E = math.log2(math.e)
F32 = jnp.float32
BF16 = jnp.bfloat16
NT = (((1,), (1,)), ((), ()))
NN = (((1,), (0,)), ((), ()))


def dot(a, b, dims):
    return lax.dot_general(a, b, dims, preferred_element_type=F32)


def lane_scan(value, reverse):
    width = value.shape[1]
    lane = lax.broadcasted_iota(jnp.int32, value.shape, 1)
    shift = 1
    while shift < width:
        if reverse:
            moved = pltpu.roll(value, width - shift, 1)
            value = value + jnp.where(lane < width - shift, moved, 0.0)
        else:
            moved = pltpu.roll(value, shift, 1)
            value = value + jnp.where(lane >= shift, moved, 0.0)
        shift *= 2
    return value


def body(
    X, Z, Y, R, D,
    q_in, k_in, v_in, g_in, o_in, gate_in, lse_in,
    dq_out, dk_out, dv_out, dgate_out,
    g_loc, o_loc, st_out,
    qst_in, kst_in, q_all, g_all, qst_all, k_all, v_all, kst_all,
    kt_all, kcol, tot_x, tot_z, pq, pk,
    dqt, row_sum, dq_own, dk_acc, dv_acc, cs_acc,
    dq_snd, dq_rcv, rs_snd, rs_rcv, dk_snd, dv_snd, dk_rcv, dv_rcv, cs_snd, cs_rcv,
    tot2_x, tot2_z, dq_fin, dk_fin, dv_fin, gs_snd, gs_rcv,
    loc_sem, p1_r, p1_s, z_r, z_s, x_r, x_s, t_r, t_s, t2_r, t2_s,
    dq_r, dq_s, rs_r, rs_s, dk_r, dk_s, f_r, f_s,
):
    H = Y * CORES
    B = H * R
    half = Z // 2
    scale = D ** -0.5
    ctx = lax.axis_index("ctx")
    y = lax.axis_index("head")
    c = ctx % CORES
    z = (ctx // CORES) % Z
    x = ctx // (CORES * Z)
    xr = X - 1 - x
    xq = jnp.where(z < half, x, xr)
    head = y * CORES + c
    part = c * Y + y

    def dev(x_, z_, c_, y_):
        return ((x_ * Z + z_) * CORES + c_, y_)

    def remote(src, dst, ssem, rsem, to):
        return pltpu.make_async_remote_copy(
            src_ref=src, dst_ref=dst, send_sem=ssem, recv_sem=rsem,
            device_id=to, device_id_type=pl.DeviceIdType.MESH,
        )

    def drain(ref, sem):
        pltpu.make_async_copy(ref, ref, sem).wait()

    loc = [
        pltpu.make_async_copy(g_in, g_loc, loc_sem.at[0]),
        pltpu.make_async_copy(o_in, o_loc, loc_sem.at[1]),
    ]
    for copy in loc:
        copy.start()

    barrier = pltpu.get_barrier_semaphore()
    group = [(dc, dy) for dy in range(Y) for dc in range(CORES)]
    partners = 0

    def greet(to):
        pl.semaphore_signal(barrier, inc=1, device_id=to, device_id_type=pl.DeviceIdType.MESH)

    for dc, dy in group:
        cc, yy = (c + dc) % CORES, (y + dy) % Y
        if (dc, dy) != (0, 0):
            greet(dev(x, z, cc, yy))
            partners += 1
        greet(dev(xr, z, cc, yy))
        partners += 1
    for d in range(1, Z):
        zz = (z + d) % Z
        greet(dev(x, zz, c, y))
        greet(dev(xr, zz, c, y))
        partners += 2
    for d in range(1, X):
        xx = (x + d) % X

        @pl.when(xx != xr)
        def _():
            greet(dev(xx, z, c, y))
    partners += X - 2
    pl.semaphore_wait(barrier, partners)

    row0 = pl.multiple_of(part * R, R)

    def to_home(src, dst, idx, to, here):
        if here is True:
            pltpu.make_async_copy(src, dst, p1_r.at[idx]).start()
        elif here is False:
            remote(src, dst, p1_s.at[idx], p1_r.at[idx], to).start()
        else:
            @pl.when(here)
            def _():
                pltpu.make_async_copy(src, dst, p1_r.at[idx]).start()

            @pl.when(jnp.logical_not(here))
            def _():
                remote(src, dst, p1_s.at[idx], p1_r.at[idx], to).start()

    def columns(h_):
        return pl.ds(pl.multiple_of(h_ * D, D), D)

    for dc, dy in group:
        cc, yy = (c + dc) % CORES, (y + dy) % Y
        hh = yy * CORES + cc
        mine = (dc, dy) == (0, 0)
        q_here = (z < half) if mine else False
        for idx, src, dst in ((0, q_in, q_all), (1, g_in, g_all)):
            to_home(src.at[:, columns(hh)], dst.at[z, pl.ds(row0, R), :], idx, dev(xq, z, cc, yy), q_here)
        for idx, src, dst in ((2, k_in, k_all), (3, v_in, v_all)):
            to_home(src.at[:, columns(hh)], dst.at[x, pl.ds(row0, R), :], idx, dev(x, z, cc, yy), mine)

    for copy in loc:
        copy.wait()
    st_out[...] = jnp.zeros_like(st_out)
    log_gate = jax.nn.log_sigmoid(gate_in[...].astype(F32)).T
    lse_t = lse_in[...].T
    for h in range(H):
        product = g_loc[:, h * D:(h + 1) * D].astype(F32) * o_loc[:, h * D:(h + 1) * D].astype(F32)
        st_out[h, 0:1, 0:R] = jnp.sum(product.T, axis=0, keepdims=True)
        st_out[h, 1:2, 0:R] = lse_t[h:h + 1, :]
        st_out[h, 2:3, 0:R] = log_gate[h:h + 1, :]
    for dc, dy in group:
        cc, yy = (c + dc) % CORES, (y + dy) % Y
        hh = yy * CORES + cc
        mine = (dc, dy) == (0, 0)
        to_home(st_out.at[hh], kst_in.at[part], 5, dev(x, z, cc, yy), mine)
        to_home(st_out.at[hh], qst_in.at[part], 4, dev(xq, z, cc, yy), (z < half) if mine else False)

    right, left = dev(x, (z + 1) % Z, c, y), dev(x, (z + Z - 1) % Z, c, y)
    ring = (q_all, qst_all, g_all)

    def hop(direction, slot, s):
        to = right if direction == 0 else left
        for arr, ref in enumerate(ring):
            last = (direction == 0) == (arr < 2)
            limit = half if last else half - 1

            @pl.when(s < limit)
            def _(arr=arr, ref=ref):
                remote(ref.at[slot], ref.at[slot], z_s.at[direction, arr, s], z_r.at[direction, arr, s], to).start()

    def hop_wait(direction, slot, s, arrs):
        for arr in arrs:
            drain(ring[arr].at[slot], z_r.at[direction, arr, s])

    def wide(tile):
        return jnp.concatenate([tile, jnp.zeros((8, B - 128), F32)], axis=1) if B > 128 else tile[:, :B]

    def assemble(ref):
        total = wide(ref[0])
        for s in range(1, H):
            total = total + pltpu.roll(wide(ref[s]), s * R, 1)
        return total

    drain(kst_in, p1_r.at[5])
    k_stats = assemble(kst_in)
    k_curve = lane_scan(k_stats, False)
    kst_all[x] = k_curve
    tot_x[x] = jnp.broadcast_to(k_curve[2:3, B - 1:B], (8, 128))
    for d in range(1, X):
        xx = (x + d) % X
        remote(tot_x.at[x], tot_x.at[x], t_s.at[0, xx], t_r.at[0, x], dev(xx, z, c, y)).start()

    drain(qst_in, p1_r.at[4])
    q_stats = assemble(qst_in)
    q_curve = lane_scan(q_stats, False)
    qst_all[z, 0:1, :] = (q_curve[2:3] - q_stats[1:2]) * LOG2E
    qst_all[z, 1:2, :] = q_stats[0:1]
    qst_all[z, 2:8, :] = jnp.zeros((6, B), F32)
    drain(q_all.at[z], p1_r.at[0])
    drain(g_all.at[z], p1_r.at[1])
    hop(0, z, 0)
    hop(1, z, 0)

    drain(k_all.at[x], p1_r.at[2])
    drain(v_all.at[x], p1_r.at[3])
    for d in range(1, X):
        xx = (x + d) % X
        to = dev(xx, z, c, y)
        for arr, ref in enumerate((k_all, v_all, kst_all)):
            remote(ref.at[x], ref.at[x], x_s.at[arr, xx], x_r.at[arr, x], to).start()

    def share_x(tot, recv):
        for d in range(1, X):
            xx = (x + d) % X
            drain(tot.at[xx], recv.at[0, xx])

    def share_z(tot, all_z, send, recv):
        all_z[z] = tot[...]
        for d in range(1, Z):
            zz = (z + d) % Z
            remote(all_z.at[z], all_z.at[z], send.at[1, zz], recv.at[1, z], dev(x, zz, c, y)).start()

    def share_end(all_z, recv):
        for d in range(1, Z):
            zz = (z + d) % Z
            drain(all_z.at[zz], recv.at[1, zz])

    share_x(tot_x, t_r)
    share_z(tot_x, tot_z, t_s, t_r)
    dk_acc[...] = jnp.zeros_like(dk_acc)
    dv_acc[...] = jnp.zeros_like(dv_acc)
    cs_acc[...] = jnp.zeros_like(cs_acc)
    for d in range(X):
        xx = (x + d) % X
        if d:
            for arr, ref in enumerate((k_all, v_all, kst_all)):
                drain(ref.at[xx], x_r.at[arr, xx])
        kt_all[xx] = k_all[xx].astype(F32).T.astype(BF16)
        column = kst_all[xx].T[:, 2:3] * LOG2E
        kcol[xx] = jnp.broadcast_to(column, (B, 128))
    share_end(tot_z, t_r)

    block_at = lax.broadcasted_iota(jnp.int32, (Z, X, 8, 128), 1) * Z + lax.broadcasted_iota(
        jnp.int32, (Z, X, 8, 128), 0
    )

    def sum_where(all_z, chosen):
        return jnp.sum(jnp.where(chosen, all_z[...], 0.0), axis=(0, 1))

    def slot_x(slot):
        return jnp.where(slot < half, x, xr)

    def fill_pq(slot, carry):
        pq[slot] = sum_where(tot_z, block_at < slot_x(slot) * Z + slot) * LOG2E
        return carry

    def fill_pk(kb, carry):
        pk[kb] = sum_where(tot_z, block_at < kb * Z + z) * LOG2E
        return carry

    lax.fori_loop(0, Z, fill_pq, 0)
    lax.fori_loop(0, X, fill_pk, 0)

    def lanes(value, width):
        return value[:, :width] if width <= 128 else jnp.concatenate([value] * (width // 128), axis=1)

    def pair(slot, kb, masked):
        k_blk, v_blk = k_all[kb], v_all[kb]
        q_blk, g_blk = q_all[slot], g_all[slot]
        away = pq[slot, 0:1, :] - pk[kb, 0:1, :]
        row = qst_all[slot, 0:1, :] + lanes(away, B)
        delta = qst_all[slot, 1:2, :]
        s = dot(k_blk, q_blk, NT)
        prob = jnp.exp2(s * (scale * LOG2E) + row - lanes(kcol[kb], B))
        if masked:
            key_at = lax.broadcasted_iota(jnp.int32, (B, B), 0)
            query_at = lax.broadcasted_iota(jnp.int32, (B, B), 1)
            prob = jnp.where(key_at <= query_at, prob, 0.0)
        grad = prob * (dot(v_blk, g_blk, NT) - delta)
        prob_half, grad_half = prob.astype(BF16), grad.astype(BF16)
        dv_acc[kb] += dot(prob_half, g_blk, NN)
        dk_acc[kb] += dot(grad_half, q_blk, NN)
        dqt[...] += dot(kt_all[kb], grad_half, NN)
        row_sum[0:1, :] += jnp.sum(grad, axis=0, keepdims=True)
        if B > 128:
            folded = grad[:, 0:128]
            for at in range(128, B, 128):
                folded = folded + grad[:, at:at + 128]
            cs_acc[kb] += folded
        else:
            cs_acc[kb, :, 0:B] += grad

    def dq_copy(slot):
        return remote(dq_snd.at[slot], dq_rcv.at[z], dq_s.at[slot], dq_r.at[z], dev(x, slot, c, y))

    def rs_copy(slot):
        return remote(rs_snd.at[slot], rs_rcv.at[z], rs_s.at[slot], rs_r.at[z], dev(slot_x(slot), slot, c, y))

    def one_slot(t, carry):
        s = (t + 1) // 2
        odd = t % 2 == 1
        slot = (jnp.where(odd, z - s, z + s) + Z) % Z

        @pl.when(jnp.logical_and(odd, s < half))
        def _():
            hop_wait(0, slot, s - 1, (0, 1, 2))
            hop(0, slot, s)
            other = (z + s) % Z
            hop_wait(1, other, s - 1, (0, 1, 2))
            hop(1, other, s)

        @pl.when(t == Z - 1)
        def _():
            hop_wait(0, slot, s - 1, (0, 1))
            hop_wait(1, slot, s - 1, (2,))

        at_x = slot_x(slot)
        dqt[...] = jnp.zeros_like(dqt)
        row_sum[...] = jnp.zeros_like(row_sum)
        full = at_x + jnp.where(z < slot, 1, 0)

        def one_pair(kb, inner):
            pair(slot, kb, False)
            return inner

        lax.fori_loop(0, full, one_pair, 0)

        @pl.when(slot == z)
        def _():
            pair(slot, at_x, True)

        rs_snd[slot] = row_sum[...]
        dq_now = dqt[...].T * scale

        @pl.when(slot == z)
        def _():
            dq_own[...] = dq_now

        @pl.when(slot != z)
        def _():
            dq_snd[slot] = dq_now.astype(BF16)
            dq_copy(slot).start()

        here = jnp.logical_and(slot == z, at_x == x)

        @pl.when(here)
        def _():
            pltpu.make_async_copy(rs_snd.at[slot], rs_rcv.at[z], rs_r.at[z]).start()

        @pl.when(jnp.logical_not(here))
        def _():
            rs_copy(slot).start()

        return carry

    lax.fori_loop(0, Z, one_slot, 0)

    def cs_lanes(kb):
        return jnp.broadcast_to(jnp.sum(cs_acc[kb].T, axis=0, keepdims=True), (8, B))

    for d in range(1, X):
        xx = (x + d) % X
        to = dev(xx, z, c, y)
        dk_snd[xx] = (dk_acc[xx] * scale).astype(BF16)
        dv_snd[xx] = dv_acc[xx].astype(BF16)
        cs_snd[xx] = cs_lanes(xx)
        for arr, (snd, rcv) in enumerate(((dk_snd, dk_rcv), (dv_snd, dv_rcv), (cs_snd, cs_rcv))):
            remote(snd.at[xx], rcv.at[x], dk_s.at[arr, xx], dk_r.at[arr, x], to).start()

    def give_back(value_ref, out_ref, idx, at_x, always_here):
        for dc, dy in group:
            cc, yy = (c + dc) % CORES, (y + dy) % Y
            src = value_ref.at[pl.ds(pl.multiple_of((cc * Y + yy) * R, R), R), :]
            dst = out_ref.at[:, columns(head)]
            to = dev(at_x, z, cc, yy)
            mine = (dc, dy) == (0, 0)
            if mine and always_here:
                pltpu.make_async_copy(src, dst, f_r.at[idx]).start()
            elif mine:
                @pl.when(at_x == x)
                def _(src=src, dst=dst):
                    pltpu.make_async_copy(src, dst, f_r.at[idx]).start()

                @pl.when(at_x != x)
                def _(src=src, dst=dst, to=to):
                    remote(src, dst, f_s.at[idx], f_r.at[idx], to).start()
            else:
                remote(src, dst, f_s.at[idx], f_r.at[idx], to).start()

    dq_sum = dq_own[...]
    for d in range(1, Z):
        zz = (z + d) % Z
        drain(dq_rcv.at[zz], dq_r.at[zz])
        dq_sum = dq_sum + dq_rcv[zz].astype(F32)
    dq_fin[...] = dq_sum.astype(BF16)
    give_back(dq_fin, dq_out, 0, xq, False)

    rows = jnp.zeros((8, B), F32)
    for d in range(Z):
        zz = (z + d) % Z
        drain(rs_rcv.at[zz], rs_r.at[zz])
        rows = rows + rs_rcv[zz]
    columns_sum = cs_lanes(x)
    dk_sum = dk_acc[x] * scale
    dv_sum = dv_acc[x]
    for d in range(1, X):
        xx = (x + d) % X
        drain(cs_rcv.at[xx], dk_r.at[2, xx])
        columns_sum = columns_sum + cs_rcv[xx]
    curve_grad = jnp.broadcast_to(rows[0:1], (8, B)) - columns_sum
    later = lane_scan(curve_grad, True)
    tot2_x[x] = jnp.broadcast_to(later[:, 0:1], (8, 128))
    for d in range(1, X):
        xx = (x + d) % X
        remote(tot2_x.at[x], tot2_x.at[x], t2_s.at[0, xx], t2_r.at[0, x], dev(xx, z, c, y)).start()
    for d in range(1, X):
        xx = (x + d) % X
        drain(dk_rcv.at[xx], dk_r.at[0, xx])
        dk_sum = dk_sum + dk_rcv[xx].astype(F32)
        drain(dv_rcv.at[xx], dk_r.at[1, xx])
        dv_sum = dv_sum + dv_rcv[xx].astype(F32)
    share_x(tot2_x, t2_r)
    share_z(tot2_x, tot2_z, t2_s, t2_r)
    dk_fin[...] = dk_sum.astype(BF16)
    give_back(dk_fin, dk_out, 1, x, True)
    dv_fin[...] = dv_sum.astype(BF16)
    give_back(dv_fin, dv_out, 2, x, True)
    share_end(tot2_z, t2_r)
    after = sum_where(tot2_z, block_at > x * Z + z)
    gate_sum = later + lanes(after, B)
    for s in range(H):
        moved = pltpu.roll(gate_sum, (B - s * R) % B, 1) if s else gate_sum
        gs_snd[s] = moved[:, 0:128] if B >= 128 else jnp.concatenate([moved, jnp.zeros((8, 128 - B), F32)], axis=1)
    for dc, dy in group:
        cc, yy = (c + dc) % CORES, (y + dy) % Y
        src, dst = gs_snd.at[cc * Y + yy], gs_rcv.at[head]
        if (dc, dy) == (0, 0):
            pltpu.make_async_copy(src, dst, f_r.at[3]).start()
        else:
            remote(src, dst, f_s.at[3], f_r.at[3], dev(x, z, cc, yy)).start()
    drain(gs_rcv, f_r.at[3])
    sub = lax.broadcasted_iota(jnp.int32, (8, 128), 0)
    by_head = jnp.zeros((8, 128), F32)
    for h in range(H):
        by_head = by_head + jnp.where(sub == h, gs_rcv[h], 0.0)
    gate_t = by_head.T[0:R, 0:H]
    dgate_out[...] = (gate_t * jax.nn.sigmoid(-gate_in[...].astype(F32))).astype(BF16)

    drain(dq_out, f_r.at[0])
    drain(dk_out, f_r.at[1])
    drain(dv_out, f_r.at[2])
    for d in range(1, X):
        xx = (x + d) % X
        for arr, ref in enumerate((k_all, v_all, kst_all)):
            drain(ref.at[x], x_s.at[arr, xx])
        for arr, ref in enumerate((dk_snd, dv_snd, cs_snd)):
            drain(ref.at[xx], dk_s.at[arr, xx])
        drain(tot_x.at[x], t_s.at[0, xx])
        drain(tot2_x.at[x], t2_s.at[0, xx])
    for d in range(1, Z):
        zz = (z + d) % Z
        drain(tot_z.at[z], t_s.at[1, zz])
        drain(tot2_z.at[z], t2_s.at[1, zz])
        drain(dq_snd.at[zz], dq_s.at[zz])
        drain(rs_snd.at[zz], rs_s.at[zz])

    @pl.when(xq != x)
    def _():
        drain(rs_snd.at[z], rs_s.at[z])

    for s in range(half):
        for direction in range(2):
            for arr, ref in enumerate(ring):
                last = (direction == 0) == (arr < 2)
                if s < (half if last else half - 1):
                    slot = (z - s + Z) % Z if direction == 0 else (z + s) % Z
                    drain(ref.at[slot], z_s.at[direction, arr, s])
    few, full = pl.ds(0, B - R), pl.ds(0, B)
    drain(k_all.at[x, few, :], p1_s.at[2])
    drain(v_all.at[x, few, :], p1_s.at[3])
    drain(kst_in.at[pl.ds(0, H - 1)], p1_s.at[5])
    drain(dk_fin.at[few, :], f_s.at[1])
    drain(dv_fin.at[few, :], f_s.at[2])
    drain(gs_snd.at[pl.ds(0, H - 1)], f_s.at[3])

    @pl.when(z < half)
    def _():
        drain(q_all.at[z, few, :], p1_s.at[0])
        drain(g_all.at[z, few, :], p1_s.at[1])
        drain(qst_in.at[pl.ds(0, H - 1)], p1_s.at[4])
        drain(dq_fin.at[few, :], f_s.at[0])

    @pl.when(z >= half)
    def _():
        drain(q_all.at[z, full, :], p1_s.at[0])
        drain(g_all.at[z, full, :], p1_s.at[1])
        drain(qst_in, p1_s.at[4])
        drain(dq_fin.at[full, :], f_s.at[0])


def plane(contexts):
    chips = contexts // CORES
    along_x = 1
    while 2 * along_x * 2 * along_x * 2 <= chips * 2 and along_x * 2 * 2 <= chips:
        along_x *= 2
    return along_x, chips // along_x


def per_device(X, Z, Y, *args):
    R, columns = args[0].shape
    H = Y * CORES
    D = columns // H
    B = H * R
    half = Z // 2
    vm = pltpu.VMEM
    dma = pltpu.SemaphoreType.DMA
    any_spec = pl.BlockSpec(memory_space=pl.ANY)
    vm_spec = pl.BlockSpec(memory_space=pltpu.VMEM)
    scratch = [
        vm((R, columns), BF16), vm((R, columns), BF16), vm((H, 8, 128), F32),
        vm((H, 8, 128), F32), vm((H, 8, 128), F32),
        vm((Z, B, D), BF16), vm((Z, B, D), BF16), vm((Z, 8, B), F32),
        vm((X, B, D), BF16), vm((X, B, D), BF16), vm((X, 8, B), F32),
        vm((X, D, B), BF16), vm((X, B, 128), F32),
        vm((X, 8, 128), F32), vm((Z, X, 8, 128), F32), vm((Z, 8, 128), F32), vm((X, 8, 128), F32),
        vm((D, B), F32), vm((8, B), F32), vm((B, D), F32),
        vm((X, B, D), F32), vm((X, B, D), F32), vm((X, B, 128), F32),
        vm((Z, B, D), BF16), vm((Z, B, D), BF16), vm((Z, 8, B), F32), vm((Z, 8, B), F32),
        vm((X, B, D), BF16), vm((X, B, D), BF16), vm((X, B, D), BF16), vm((X, B, D), BF16),
        vm((X, 8, B), F32), vm((X, 8, B), F32),
        vm((X, 8, 128), F32), vm((Z, X, 8, 128), F32),
        vm((B, D), BF16), vm((B, D), BF16), vm((B, D), BF16),
        vm((H, 8, 128), F32), vm((H, 8, 128), F32),
        dma((2,)), dma((6,)), dma((6,)), dma((2, 3, half)), dma((2, 3, half)),
        dma((3, X)), dma((3, X)), dma((2, Z)), dma((2, Z)), dma((2, Z)), dma((2, Z)),
        dma((Z,)), dma((Z,)), dma((Z,)), dma((Z,)), dma((3, X)), dma((3, X)), dma((4,)), dma((4,)),
    ]
    big = jax.ShapeDtypeStruct((R, columns), BF16)
    return pl.pallas_call(
        functools.partial(body, X, Z, Y, R, D),
        out_shape=(big, big, big, jax.ShapeDtypeStruct((R, H), BF16)),
        in_specs=[any_spec] * 5 + [vm_spec] * 2,
        out_specs=(any_spec, any_spec, any_spec, vm_spec),
        scratch_shapes=scratch,
        compiler_params=pltpu.CompilerParams(
            collective_id=0, has_side_effects=True, vmem_limit_bytes=48 * 1024 * 1024
        ),
    )(*args)


def solution(mesh):
    X, Z = plane(mesh.shape["ctx"])
    Y = mesh.shape["head"]
    rows = P(("ctx", "head"), None)
    return jax.shard_map(
        functools.partial(per_device, X, Z, Y),
        mesh=mesh,
        in_specs=(rows,) * 7,
        out_specs=(rows,) * 4,
        check_vma=False,
    )
```

time: 591 us -> 96.7 us (0.16)
  blocking collectives: 341 us -> 0 us
  Pallas kernels: 0 us -> 87.9 us
  waiting for transfers between devices: 71.5 us -> 0 us
  local copies, waits for them, and re-layouts: 79.2 us -> 7.9 us
  matrix products: 31.7 us -> 0 us
  starting transfers between devices: 29.4 us -> 0 us
  between operations: 14.7 us -> 0.66 us
  other arithmetic: 9.45 us -> 0 us
  loops' own time: 7.85 us -> 0 us
    all_gather x4 -> x0, blocking collectives: 193 us -> none  [the longest x1 48.6 us: prefix(): everything = lax.all_gather(value, axis)]
    unnamed x1 -> x0, blocking collectives: 124 us -> none
    pallas_call x0 -> x1, Pallas kernels: none -> 87.9 us  [per_device(): pl.pallas_call(functools.partial(body, X, Z, Y, R, D), out_shape=(big, bi...]
    all_gather x4 -> x0, waiting for transfers between devices: 54.1 us -> none  [the longest x1 54.1 us: per_device(): lax.all_gather(my_grad, 'ctx', axis=0, tiled=True)]
    dot_general x99 -> x0, matrix products: 31.7 us -> none  [the longest x25 9.52 us: block_scores(): jnp.einsum('qhd,khd->hqk', query_blk, key_blk, preferred_element_type=jnp...]
    unnamed x29 -> x17, local copies, waits for them, and re-layouts: 37.8 us -> 7.24 us
    all_to_all x8 -> x0, starting transfers between devices: 29.2 us -> none  [the longest x1 4.52 us: per_device(): lax.all_to_all(attn_output, 'head', split_axis=1, concat_axis=0, tiled=True)]
    dynamic_slice x26 -> x0, local copies, waits for them, and re-layouts: 26.9 us -> none  [the longest x25 26.8 us: one_turn(): lax.dynamic_slice_in_dim(member, offset, block_len, 0)]
  transfers between devices with their start and end apart: 12 -> 0, of which waited for: 6 -> 0; matrix products, arithmetic and copies ran while one was open for 8% -> 0% of each run, Pallas kernels for 0% -> 0%
where the time goes in v1:
time: 96.7 us; the launch traced here: 96.5 us
  Pallas kernels  87.9 us (91%)
  local copies, waits for them, and re-layouts  7.9 us (8%)
    pallas_call x1, Pallas kernels, per_device(): pl.pallas_call(functools.partial(body, X, Z, Y, R, D), out_shape=(big, bi...  87.9 us
    unnamed x17, local copies, waits for them, and re-layouts  7.24 us

profile of v1, /device:TPU:1, one launch (start us, length us, event | category | flops | bytes accessed | tf_op | source)
XLA Modules:
  0.0 96.5 jit_solution(506414142793633032)
XLA Ops:
  0.6 0.0 copy-start.5
  0.6 0.8 copy.11.gate_in
  1.4 0.0 copy-done.5
  1.4 0.1 copy.12.lse_in
  1.5 0.0 copy-start
  1.5 0.9 copy-done
  2.4 0.0 copy-start.1
  2.4 0.9 copy-done.1
  3.3 0.0 copy-start.2
  3.3 0.9 copy-done.2
  4.2 0.0 copy-start.3
  4.2 0.9 copy-done.3
  5.1 0.0 copy-start.4
  5.1 0.9 copy-done.4
  6.0 87.9 %shard_map.102 = (bf16[48,1024]{1,0:T(8,128)(2,1)S(1)}, bf16[48,1024]{1,0:T(8,128)(2,1)S(1)}, bf16[48,1024]{1,0:T(8,128)(2,1)S(1)}, bf16[48,8]{1,0:T(8,128)(2,1)S(1)}) custom-call(bf16[48,1024]{1,0:T(8,128)(2,1)S(1)} %copy-done, bf16[48,1024]{1,0:T(8,128)(2,1)S(1)} %copy-done.1, bf16[48,1024]{1,0:T(8,128)(2,1)S(1)} %copy-done.2, ...), custom_call_target="tpu_custom_call" | custom-call | tf_op jit(solution)/shard_map/pallas_call | solution.py:539
  93.9 0.7 copy.13
  94.5 0.6 copy.17
  95.2 0.6 copy.18
  95.8 0.6 copy.19
Async XLA Ops:
  0.6 0.8 copy-start.5
  1.5 0.9 copy-start
  2.4 0.9 copy-start.1
  3.3 0.9 copy-start.2
  4.2 0.9 copy-start.3
  5.1 0.9 copy-start.4

commit v2 on v0

v2 whole, which is shorter than its diff:
```python
import functools
import math

import jax
import jax.numpy as jnp
from jax import lax
from jax.experimental import pallas as pl
from jax.experimental.pallas import tpu as pltpu
from jax.sharding import PartitionSpec as P

CORES = 2
WIDTH = 128
LOG2E = math.log2(math.e)
F32 = jnp.float32
BF16 = jnp.bfloat16
NT = (((1,), (1,)), ((), ()))
NN = (((1,), (0,)), ((), ()))


def dot(a, b, dims):
    return lax.dot_general(a, b, dims, preferred_element_type=F32)


def iota(shape, axis):
    return lax.broadcasted_iota(jnp.int32, shape, axis)


def section_of(index, size, count):
    return sum(((index >= k * size).astype(jnp.int32) for k in range(1, count)), jnp.zeros_like(index))


def section_scan(value, size, count, reverse):
    lane = iota(value.shape, 1)
    inner = lane - size * section_of(lane, size, count)
    width, shift = value.shape[1], 1
    while shift < size:
        if reverse:
            value = value + jnp.where(inner < size - shift, pltpu.roll(value, width - shift, 1), 0.0)
        else:
            value = value + jnp.where(inner >= shift, pltpu.roll(value, shift, 1), 0.0)
        shift *= 2
    return value


def row_scan(value, reverse):
    row, rows = iota(value.shape, 0), value.shape[0]

    def moved(arr, shift):
        if reverse:
            return jnp.where(row < rows - shift, pltpu.roll(arr, rows - shift, 0), 0.0)
        return jnp.where(row >= shift, pltpu.roll(arr, shift, 0), 0.0)

    value, shift = moved(value, 1), 1
    while shift < rows:
        value = value + moved(value, shift)
        shift *= 2
    return value


def lanes(value, width):
    return value[:, :width] if width <= 128 else jnp.concatenate([value] * (width // 128), axis=1)


def body(
    X, Z, Y, R, KC,
    q_in, k_in, v_in, g_in, o_in, gate_in, lse_in,
    dq_out, dk_out, dv_out, dgate_out,
    g_loc, o_loc, gate_pad, st_out, qst_in, kst_in,
    q_all, g_all, qst_all, k_all, v_all, kst_all, kcol, kpos, tot_all, p_all,
    kt_all, q_row, dqt, dqt_own, row_acc, dk_acc, dv_acc, cs_acc,
    sib_snd, sib_rcv, dq_snd, dq_rcv, rs_snd, rs_rcv, dk_snd, dv_snd, dk_rcv, dv_rcv, cs_snd, cs_rcv,
    after_all, dq_fin, dk_fin, dv_fin, gs_snd, gs_rcv,
    loc_sem, p1_r, p1_s, x_r, x_s, y_r, y_s, sib_r, sib_s, qs_r, qs_s, ks_r, ks_s,
    t_r, t_s, dsib_r, dsib_s, dq_r, dq_s, rs_r, rs_s, dk_r, dk_s, cs_r, cs_s, f_r, f_s,
):
    D, H = WIDTH, Z
    half, CY = Z // 2, CORES * Y
    HB, B = half * R, Z * R
    scale = D ** -0.5
    ctx = lax.axis_index("ctx")
    y = lax.axis_index("head")
    c = ctx % CORES
    z = (ctx // CORES) % Z
    x = ctx // (CORES * Z)
    xr = X - 1 - x
    xk = jnp.where(z < half, x, xr)
    cy = c * Y + y
    mesh_id = pl.DeviceIdType.MESH

    def dev(x_, z_, c_, y_):
        return ((x_ * Z + z_) * CORES + c_, y_)

    def remote(src, dst, ssem, rsem, to):
        return pltpu.make_async_remote_copy(
            src_ref=src, dst_ref=dst, send_sem=ssem, recv_sem=rsem, device_id=to, device_id_type=mesh_id
        )

    def drain(ref, sem):
        pltpu.make_async_copy(ref, ref, sem).wait()

    def send(src, dst, ssem, rsem, to, here):
        if here is False:
            remote(src, dst, ssem, rsem, to).start()
        elif here is True:
            pltpu.make_async_copy(src, dst, rsem).start()
        else:
            @pl.when(here)
            def _():
                pltpu.make_async_copy(src, dst, rsem).start()

            @pl.when(jnp.logical_not(here))
            def _():
                remote(src, dst, ssem, rsem, to).start()

    loc = [
        pltpu.make_async_copy(g_in, g_loc, loc_sem.at[0]),
        pltpu.make_async_copy(o_in, o_loc, loc_sem.at[1]),
    ]
    for copy in loc:
        copy.start()

    barrier = pltpu.get_barrier_semaphore()
    plane = [(dx, dc, dy) for dx in range(X) for dc in range(CORES) for dy in range(Y)][1:]

    def greet(to):
        pl.semaphore_signal(barrier, inc=1, device_id=to, device_id_type=mesh_id)

    for d in range(1, Z):
        zz = (z + d) % Z
        greet(dev(x, zz, c, y))
        greet(dev(xr, zz, c, y))
    for dx, dc, dy in plane:
        greet(dev((x + dx) % X, z, (c + dc) % CORES, (y + dy) % Y))
    pl.semaphore_wait(barrier, 2 * (Z - 1) + len(plane))

    def columns(h_):
        return pl.ds(pl.multiple_of(h_ * D, D), D)

    z_half = z // half

    def z_rows(block):
        return pl.ds(pl.multiple_of(block * HB + (z % half) * R, R), R)

    def block_rows(block):
        return pl.ds(pl.multiple_of(block * HB, HB), HB)

    for idx, src, dst in ((0, q_in, q_all), (1, g_in, g_all), (2, k_in, k_all), (3, v_in, v_all)):
        for d in range(Z):
            zz = (z + d) % Z
            if idx < 2:
                at, to, here = dst.at[2 * x + z_half, z_rows(c), :], dev(x, zz, c, y), d == 0
            else:
                at, to = dst.at[z_half, z_rows(y), :], dev(xk, zz, c, y)
                here = (xk == x) if d == 0 else False
            send(src.at[:, columns(zz)], at, p1_s.at[idx], p1_r.at[idx], to, here)

    for copy in loc:
        copy.wait()
    st_out[...] = jnp.zeros_like(st_out)
    gate_pad[...] = jnp.zeros_like(gate_pad)
    gate_float = gate_in[...].astype(F32)
    gate_pad[0:H, 0:R] = jax.nn.log_sigmoid(gate_float)
    curve = section_scan(gate_pad[...], R, 1, False)
    lse_rows = lse_in[...]
    for h in range(H):
        cut = slice(h * D, (h + 1) * D)
        product = g_loc[:, cut].astype(F32) * o_loc[:, cut].astype(F32)
        st_out[h, 0:1, 0:R] = jnp.sum(product.T, axis=0, keepdims=True)
        st_out[h, 1:2, 0:R] = lse_rows[h:h + 1, :]
        st_out[h, 2:3, 0:R] = curve[h:h + 1, 0:R]
    for d in range(Z):
        zz = (z + d) % Z
        send(st_out.at[zz], qst_in.at[z], p1_s.at[4], p1_r.at[4], dev(x, zz, c, y), d == 0)
        send(
            st_out.at[zz], kst_in.at[z], p1_s.at[5], p1_r.at[5], dev(xk, zz, c, y),
            (xk == x) if d == 0 else False,
        )

    def q_block(ref, x_, c_):
        return ref.at[pl.ds(2 * x_, 2), block_rows(c_), :]

    def k_block(ref, y_):
        return ref.at[:, block_rows(y_), :]

    sibling = dev(x, z, 1 - c, y)
    queries = [functools.partial(q_block, ref, c_=c) for ref in (q_all, g_all)]
    keys = [functools.partial(k_block, ref) for ref in (k_all, v_all)]

    def x_dev(x_):
        return dev(x_, z, c, y)

    def y_dev(y_):
        return dev(x, z, c, y_)

    def ring_start(blocks, arr, at, n, place, snd, rcv):
        if n > 1:
            block = blocks[arr](at)
            remote(block, block, snd.at[arr, 0], rcv.at[arr, 0], place((at + 1) % n)).start()
        if n > 2:
            remote(block, block, snd.at[arr, 1], rcv.at[arr, 1], place((at + n - 1) % n)).start()

    def ring_onward(blocks, arr, at, n, place, snd, rcv):
        if n > 2:
            came, to = ((at + n - 1) % n, (at + 1) % n) if arr == 0 else ((at + 1) % n, (at + n - 1) % n)
            drain(blocks[arr](came), rcv.at[arr, arr])
            remote(blocks[arr](came), blocks[arr](came), snd.at[arr, 2], rcv.at[arr, 2], place(to)).start()
        elif n > 1:
            drain(blocks[arr]((at + 1) % n), rcv.at[arr, 0])

    def ring_other(blocks, arr, at, n, rcv):
        if n > 2:
            drain(blocks[arr]((at + 1) % n if arr == 0 else (at + n - 1) % n), rcv.at[arr, 1 - arr])

    def ring_last(blocks, arr, at, n, rcv):
        if n > 2:
            drain(blocks[arr]((at + 2) % n), rcv.at[arr, 2])

    def ring_sent(blocks, arr, at, n, snd):
        block = blocks[arr](at)
        for k in range(0 if n == 1 else 1 if n == 2 else 3):
            drain(block, snd.at[arr, k])

    def to_sibling(arr, x_):
        block = queries[arr](x_)
        remote(block, block, sib_s.at[arr, x_], sib_r.at[arr, x_], sibling).start()

    for arr in range(2):
        drain(queries[arr](x), p1_r.at[arr])
        ring_start(queries, arr, x, X, x_dev, x_s, x_r)
        to_sibling(arr, x)

    def wide(tile):
        return jnp.concatenate([tile, jnp.zeros((8, B - 128), F32)], axis=1) if B > 128 else tile[:, :B]

    def assemble(ref):
        total = wide(ref[0])
        for s in range(1, Z):
            total = total + pltpu.roll(wide(ref[s]), s * R, 1)
        return total

    row_at = iota((8, 128), 0)
    drain(qst_in, p1_r.at[4])
    totals = jnp.zeros((8, 128), F32)
    for s in range(Z):
        totals = jnp.where(row_at == s, jnp.broadcast_to(qst_in[s, 2:3, R - 1:R], (8, 128)), totals)
    tot_all[x * CY + cy] = totals

    def spread(ref, slot, semr, sems):
        for dx, dc, dy in plane:
            to = dev((x + dx) % X, z, (c + dc) % CORES, (y + dy) % Y)
            remote(ref.at[slot], ref.at[slot], sems, semr, to).start()

    spread(tot_all, x * CY + cy, t_r.at[0], t_s.at[0])
    q_stats = assemble(qst_in)
    xc = x * CORES + c
    qst_all[xc, 0:1, :] = q_stats[2:3] - q_stats[1:2]
    qst_all[xc, 1:2, :] = q_stats[0:1]
    qst_all[xc, 2:8, :] = jnp.zeros((6, B), F32)
    q_team = [(dx, dc) for dx in range(X) for dc in range(CORES)][1:]
    for dx, dc in q_team:
        x_, c_ = (x + dx) % X, (c + dc) % CORES
        mine = qst_all.at[xc]
        remote(mine, mine, qs_s.at[0], qs_r.at[0], dev(x_, z, c_, y)).start()

    drain(kst_in, p1_r.at[5])
    kst_all[y] = assemble(kst_in)
    for dy in range(1, Y):
        mine = kst_all.at[y]
        remote(mine, mine, ks_s.at[0], ks_r.at[0], y_dev((y + dy) % Y)).start()
    for arr in range(2):
        drain(keys[arr](y), p1_r.at[2 + arr])
        ring_start(keys, arr, y, Y, y_dev, y_s, y_r)

    dk_acc[...] = jnp.zeros_like(dk_acc)
    dv_acc[...] = jnp.zeros_like(dv_acc)
    cs_acc[...] = jnp.zeros_like(cs_acc)
    dqt[...] = jnp.zeros_like(dqt)
    row_acc[...] = jnp.zeros_like(row_acc)
    k_at = iota((Y * HB, 128), 0)
    k_y = section_of(k_at, HB, Y)
    k_rest = k_at - HB * k_y
    k_z = section_of(k_rest, R, half)
    kpos[...] = k_z * (CY * R) + c * (Y * R) + k_y * R + (k_rest - R * k_z)
    q_at = iota((8, B), 1)
    q_c = section_of(q_at, HB, CORES)
    q_rest = q_at - HB * q_c
    q_z = section_of(q_rest, R, half)
    qpos = q_z * (CY * R) + q_c * (Y * R) + y * R + (q_rest - R * q_z)

    for arr in range(2):
        ring_onward(queries, arr, x, X, x_dev, x_s, x_r)
        if X > 1:
            to_sibling(arr, (x + X - 1) % X if arr == 0 or X == 2 else (x + 1) % X)
    for arr in range(2):
        ring_onward(keys, arr, y, Y, y_dev, y_s, y_r)
    if X > 2:
        for arr in range(2):
            ring_other(queries, arr, x, X, x_r)
            to_sibling(arr, (x + 1) % X if arr == 0 else (x + X - 1) % X)

    few = X * CY - 1
    drain(tot_all.at[pl.ds(0, few)], t_r.at[0])
    before = jnp.zeros((8, 128), F32)
    for x_ in range(X):
        level = jnp.zeros((8, 128), F32)
        for k in range(CY):
            level = level + tot_all[x_ * CY + k]
        run = before + row_scan(level, False)
        for k in range(CY):
            p_all[x_ * CY + k] = run
            run = run + tot_all[x_ * CY + k]
        before = before + jnp.sum(level, axis=0, keepdims=True)

    piece_row, piece_lane = iota((8, B), 0), iota((8, B), 1)
    in_piece = piece_row == section_of(piece_lane, R, Z)

    def along_lanes(tile):
        return jnp.sum(jnp.where(in_piece, lanes(tile, B), 0.0), axis=0, keepdims=True)

    low = iota((8, B), 1) < HB

    def halves(first, second):
        return (
            jnp.where(low, first, pltpu.roll(second, HB, 1)),
            jnp.where(low, pltpu.roll(first, HB, 1), second),
        )

    drain(qst_all.at[pl.ds(0, len(q_team))], qs_r.at[0])
    for x_ in range(X):
        rows = []
        for c_ in range(CORES):
            bias = along_lanes(p_all[x_ * CY + c_ * Y + y])
            stat = qst_all[x_ * CORES + c_]
            rows.append(jnp.where(iota((8, B), 0) == 0, (stat + bias) * LOG2E, stat))
        lo, hi = halves(*rows)
        q_row[2 * x_] = lo
        q_row[2 * x_ + 1] = hi

    if Y > 1:
        drain(kst_all.at[pl.ds(0, Y - 1)], ks_r.at[0])
    for y_ in range(Y):
        tile = jnp.where(row_at < half, p_all[x * CY + c * Y + y_], p_all[xr * CY + c * Y + y_])
        column = ((kst_all[y_] + along_lanes(tile)) * LOG2E).T[:, 2:3]
        spread_column = jnp.broadcast_to(column, (B, 128))
        kcol[0, y_ * HB:(y_ + 1) * HB, :] = spread_column[0:HB]
        kcol[1, y_ * HB:(y_ + 1) * HB, :] = spread_column[HB:B]

    for arr in range(2):
        ring_other(keys, arr, y, Y, y_r)
    for arr in range(2):
        ring_last(keys, arr, y, Y, y_r)
    if X > 2:
        for arr in range(2):
            ring_last(queries, arr, x, X, x_r)
            to_sibling(arr, (x + 2) % X)
    for arr in range(2):
        for x_ in range(X):
            drain(q_block(q_all, x_, 1 - c), sib_r.at[arr, x_])

    def pair(u, kh, masked):
        q_blk, g_blk, stat = q_all[u], g_all[u], q_row[u]
        row, delta = stat[0:1], stat[1:2]

        def chunk(k, carry):
            at = pl.ds(pl.multiple_of(k * KC, KC), KC)
            k_blk, v_blk = k_all[kh, at, :], v_all[kh, at, :]
            s = dot(k_blk, q_blk, NT)
            prob = jnp.exp2(s * (scale * LOG2E) + row - lanes(kcol[kh, at, :], B))
            if masked:
                prob = jnp.where(lanes(kpos[at, :], B) <= qpos[0:1], prob, 0.0)
            grad = prob * (dot(v_blk, g_blk, NT) - delta)
            prob_half, grad_half = prob.astype(BF16), grad.astype(BF16)
            dv_acc[kh, at, :] += dot(prob_half, g_blk, NN)
            dk_acc[kh, at, :] += dot(grad_half, q_blk, NN)
            dqt[u] += dot(kt_all[kh, k], grad_half, NN)
            row_acc[u, 0:1, :] += jnp.sum(grad, axis=0, keepdims=True)
            if B > 128:
                folded = grad[:, 0:128]
                for lane in range(128, B, 128):
                    folded = folded + grad[:, lane:lane + 128]
                cs_acc[kh, at, :] += folded
            else:
                cs_acc[kh, at, 0:B] += grad
            return carry

        lax.fori_loop(0, Y * HB // KC, chunk, 0)

    for kh in range(2):
        for k in range(Y * HB // KC):
            kt_all[kh, k] = k_all[kh, k * KC:(k + 1) * KC, :].astype(F32).T.astype(BF16)
    for kh in range(2):
        first = 2 * x if kh == 0 else 2 * xr + 1
        pair(first, kh, True)

        def one(u, carry, kh=kh):
            pair(u, kh, False)
            return carry

        lax.fori_loop(first + 1, 2 * X, one, 0)

    for x_ in range(X):
        lo, hi = halves(row_acc[2 * x_], row_acc[2 * x_ + 1])
        for c_, tile in ((0, lo), (1, hi)):
            rs_snd[x_ * CORES + c_] = tile

    def team(dx, dc):
        return (x + dx) % X, (c + dc) % CORES

    for dx, dc in [(0, 0)] + q_team:
        x_, c_ = team(dx, dc)
        send(
            rs_snd.at[x_ * CORES + c_], rs_rcv.at[xc], rs_s.at[0], rs_r.at[0], dev(x_, z, c_, y), (dx, dc) == (0, 0)
        )
    for y_ in range(Y):
        rows = pl.ds(y_ * HB, HB)
        column = jnp.concatenate([cs_acc[0, rows, :], cs_acc[1, rows, :]], axis=0)
        cs_snd[y_] = jnp.broadcast_to(jnp.sum(column.T, axis=0, keepdims=True), (8, B))
    for dy in range(Y):
        y_ = (y + dy) % Y
        send(cs_snd.at[y_], cs_rcv.at[0, y], cs_s.at[0], cs_r.at[0], y_dev(y_), dy == 0)
        send(cs_snd.at[y_], cs_rcv.at[1, y], cs_s.at[1], cs_r.at[1], dev(xr, z, c, y_), False)

    for dx in range(X):
        x_ = (x + dx) % X
        for hf in range(2):
            dqt_unit = dqt[2 * x_ + hf].T * scale
            lower, upper = dqt_unit[0:HB], dqt_unit[HB:B]
            mine = jnp.where(c == 0, lower, upper)
            theirs = jnp.where(c == 0, upper, lower)
            sib_snd[x_, hf] = theirs.astype(BF16)
            dqt_own[x_, hf] = mine
        remote(sib_snd.at[x_], sib_rcv.at[x_], dsib_s.at[x_], dsib_r.at[x_], sibling).start()

    for dy in range(1, Y):
        y_ = (y + dy) % Y
        rows = block_rows(y_)
        for kh in range(2):
            dk_snd[y_, kh] = (dk_acc[kh, rows, :] * scale).astype(BF16)
            dv_snd[y_, kh] = dv_acc[kh, rows, :].astype(BF16)
        remote(dk_snd.at[y_], dk_rcv.at[y], dk_s.at[0, y_], dk_r.at[0, y], y_dev(y_)).start()
        remote(dv_snd.at[y_], dv_rcv.at[y], dk_s.at[1, y_], dk_r.at[1, y], y_dev(y_)).start()

    for dx in range(1, X):
        x_ = (x + dx) % X
        drain(sib_rcv.at[x_], dsib_r.at[x_])
        dq_snd[x_] = (dqt_own[x_] + sib_rcv[x_].astype(F32)).astype(BF16)
        remote(dq_snd.at[x_], dq_rcv.at[x], dq_s.at[x_], dq_r.at[x], x_dev(x_)).start()

    drain(rs_rcv, rs_r.at[0])
    drain(cs_rcv.at[0], cs_r.at[0])
    drain(cs_rcv.at[1], cs_r.at[1])
    rows_sum = jnp.zeros((8, B), F32)
    for x_ in range(X):
        for c_ in range(CORES):
            rows_sum = rows_sum + rs_rcv[x_ * CORES + c_]
    columns_sum = jnp.zeros((8, B), F32)
    for y_ in range(Y):
        columns_sum = columns_sum + jnp.where(low, cs_rcv[0, y_], cs_rcv[1, y_])
    later = section_scan(jnp.broadcast_to(rows_sum[0:1], (8, B)) - columns_sum, R, Z, True)
    totals = jnp.zeros((8, 128), F32)
    for s in range(Z):
        totals = jnp.where(row_at == s, jnp.broadcast_to(later[0:1, s * R:s * R + 1], (8, 128)), totals)
    after_all[x * CY + cy] = totals
    spread(after_all, x * CY + cy, t_r.at[1], t_s.at[1])

    def give_back(fin, out, idx, keyed):
        for d in range(Z):
            zz = (z + d) % Z
            src = fin.at[zz // half, pl.ds(pl.multiple_of((zz % half) * R, R), R), :]
            dst = out.at[:, columns(z)]
            at_x = jnp.where(zz < half, x, xr) if keyed else x
            here = False if d else ((at_x == x) if keyed else True)
            send(src, dst, f_s.at[idx], f_r.at[idx], dev(at_x, zz, c, y), here)

    for rcv, acc, fin, out, idx, factor in (
        (dk_rcv, dk_acc, dk_fin, dk_out, 1, scale), (dv_rcv, dv_acc, dv_fin, dv_out, 2, 1.0)
    ):
        own = block_rows(y)
        sums = [acc[kh, own, :] * factor for kh in range(2)]
        for dy in range(1, Y):
            y_ = (y + dy) % Y
            drain(rcv.at[y_], dk_r.at[idx - 1, y_])
            sums = [sums[kh] + rcv[y_, kh].astype(F32) for kh in range(2)]
        for kh in range(2):
            fin[kh] = sums[kh].astype(BF16)
        give_back(fin, out, idx, True)

    drain(sib_rcv.at[x], dsib_r.at[x])
    dq_sum = dqt_own[x] + sib_rcv[x].astype(F32)
    for dx in range(1, X):
        x_ = (x + dx) % X
        drain(dq_rcv.at[x_], dq_r.at[x_])
        dq_sum = dq_sum + dq_rcv[x_].astype(F32)
    dq_fin[...] = dq_sum.astype(BF16)
    give_back(dq_fin, dq_out, 0, False)

    drain(after_all.at[pl.ds(0, few)], t_r.at[1])
    after = jnp.zeros((8, 128), F32)
    for x_ in range(X):
        level = jnp.zeros((8, 128), F32)
        for k in range(CY):
            tile = after_all[x_ * CY + k]
            level = level + tile
            after = after + jnp.where(jnp.logical_and(x_ == x, k > cy), tile, 0.0)
        after = after + jnp.where(x_ == x, row_scan(level, True), 0.0)
        after = after + jnp.where(x_ > x, jnp.sum(level, axis=0, keepdims=True), 0.0)
    gate_sum = later + along_lanes(after)
    for s in range(Z):
        moved = pltpu.roll(gate_sum, (B - s * R) % B, 1) if s else gate_sum
        gs_snd[s] = moved[:, 0:128] if B >= 128 else jnp.concatenate([moved, jnp.zeros((8, 128 - B), F32)], axis=1)
    for d in range(Z):
        zz = (z + d) % Z
        send(gs_snd.at[zz], gs_rcv.at[z], f_s.at[3], f_r.at[3], dev(x, zz, c, y), d == 0)
    drain(gs_rcv, f_r.at[3])
    by_head = jnp.zeros((8, 128), F32)
    for h in range(H):
        by_head = by_head + jnp.where(row_at == h, gs_rcv[h], 0.0)
    dgate_out[...] = (by_head[0:H, 0:R] * jax.nn.sigmoid(-gate_float)).astype(BF16)

    for arr in range(2):
        ring_sent(queries, arr, x, X, x_s)
        ring_sent(keys, arr, y, Y, y_s)
        for x_ in range(X):
            drain(queries[arr](x_), sib_s.at[arr, x_])
        for dy in range(1, Y):
            y_ = (y + dy) % Y
            drain(dk_snd.at[y_], dk_s.at[arr, y_])
    drain(qst_all.at[pl.ds(0, len(q_team))], qs_s.at[0])
    drain(rs_snd.at[pl.ds(0, len(q_team))], rs_s.at[0])
    if Y > 1:
        drain(kst_all.at[pl.ds(0, Y - 1)], ks_s.at[0])
        drain(cs_snd.at[pl.ds(0, Y - 1)], cs_s.at[0])
    drain(cs_snd, cs_s.at[1])
    drain(tot_all.at[pl.ds(0, few)], t_s.at[0])
    drain(after_all.at[pl.ds(0, few)], t_s.at[1])
    for dx in range(X):
        x_ = (x + dx) % X
        drain(sib_snd.at[x_], dsib_s.at[x_])
        if dx:
            drain(dq_snd.at[x_], dq_s.at[x_])

    for idx in range(4):
        less, more = q_in.at[:, pl.ds(0, (Z - 1) * D)], q_in
        if idx < 2:
            drain(less, p1_s.at[idx])
        else:
            @pl.when(xk == x)
            def _(idx=idx, less=less):
                drain(less, p1_s.at[idx])

            @pl.when(xk != x)
            def _(idx=idx, more=more):
                drain(more, p1_s.at[idx])
    drain(qst_in.at[pl.ds(0, Z - 1)], p1_s.at[4])
    drain(gs_snd.at[pl.ds(0, Z - 1)], f_s.at[3])

    @pl.when(xk == x)
    def _():
        drain(kst_in.at[pl.ds(0, Z - 1)], p1_s.at[5])
        drain(q_in.at[:, pl.ds(0, (Z - 1) * D)], f_s.at[1])
        drain(q_in.at[:, pl.ds(0, (Z - 1) * D)], f_s.at[2])

    @pl.when(xk != x)
    def _():
        drain(kst_in, p1_s.at[5])
        drain(q_in, f_s.at[1])
        drain(q_in, f_s.at[2])

    drain(q_in.at[:, pl.ds(0, (Z - 1) * D)], f_s.at[0])
    drain(dq_out, f_r.at[0])
    drain(dk_out, f_r.at[1])
    drain(dv_out, f_r.at[2])


def per_device(X, Y, *args):
    R, columns = args[0].shape
    D, Z, C = WIDTH, columns // WIDTH, CORES
    HB, B, H = Z // 2 * R, Z * R, Z
    KC = min(256, Y * HB)
    vm = pltpu.VMEM
    dma = pltpu.SemaphoreType.DMA
    any_spec = pl.BlockSpec(memory_space=pl.ANY)
    vm_spec = pl.BlockSpec(memory_space=pltpu.VMEM)
    queries, keys = (2 * X, C * HB, D), (2, Y * HB, D)
    block, tile = (2, HB, D), (8, 128)
    scratch = [
        vm((R, columns), BF16), vm((R, columns), BF16), vm(tile, F32),
        vm((H,) + tile, F32), vm((Z,) + tile, F32), vm((Z,) + tile, F32),
        vm(queries, BF16), vm(queries, BF16), vm((X * C, 8, B), F32),
        vm(keys, BF16), vm(keys, BF16), vm((Y, 8, B), F32),
        vm((2, Y * HB, 128), F32), vm((Y * HB, 128), jnp.int32),
        vm((X * C * Y,) + tile, F32), vm((X * C * Y,) + tile, F32),
        vm((2, Y * HB // KC, D, KC), BF16), vm((2 * X, 8, B), F32),
        vm((2 * X, D, B), F32), vm((X,) + block, F32), vm((2 * X, 8, B), F32),
        vm(keys, F32), vm(keys, F32), vm((2, Y * HB, 128), F32),
        vm((X,) + block, BF16), vm((X,) + block, BF16), vm((X,) + block, BF16), vm((X,) + block, BF16),
        vm((X * C, 8, B), F32), vm((X * C, 8, B), F32),
        vm((Y,) + block, BF16), vm((Y,) + block, BF16), vm((Y,) + block, BF16), vm((Y,) + block, BF16),
        vm((Y, 8, B), F32), vm((2, Y, 8, B), F32),
        vm((X * C * Y,) + tile, F32), vm(block, BF16), vm(block, BF16), vm(block, BF16),
        vm((Z,) + tile, F32), vm((H,) + tile, F32),
        dma((2,)), dma((6,)), dma((6,)), dma((2, 3)), dma((2, 3)), dma((2, 3)), dma((2, 3)),
        dma((2, X)), dma((2, X)), dma((1,)), dma((1,)), dma((1,)), dma((1,)),
        dma((2,)), dma((2,)), dma((X,)), dma((X,)), dma((X,)), dma((X,)), dma((1,)), dma((1,)),
        dma((2, Y)), dma((2, Y)), dma((2,)), dma((2,)), dma((4,)), dma((4,)),
    ]
    big = jax.ShapeDtypeStruct((R, columns), BF16)
    dq, dk, dv, dgate = pl.pallas_call(
        functools.partial(body, X, Z, Y, R, KC),
        out_shape=(big, big, big, jax.ShapeDtypeStruct((H, R), BF16)),
        in_specs=[any_spec] * 5 + [vm_spec] * 2,
        out_specs=(any_spec, any_spec, any_spec, vm_spec),
        scratch_shapes=scratch,
        compiler_params=pltpu.CompilerParams(
            collective_id=0, has_side_effects=True, vmem_limit_bytes=63 * 1024 * 1024
        ),
    )(*args[:5], args[5].T, args[6].T)
    return dq, dk, dv, dgate.T


def solution(mesh):
    rows = P(("ctx", "head"), None)

    def whole(*args):
        X = mesh.shape["ctx"] // (CORES * (args[0].shape[1] // WIDTH))
        return jax.shard_map(
            functools.partial(per_device, X, mesh.shape["head"]),
            mesh=mesh,
            in_specs=(rows,) * 7,
            out_specs=(rows,) * 4,
            check_vma=False,
        )(*args)

    return whole
```

time: 591 us -> 78.5 us (0.13)
  blocking collectives: 341 us -> 0 us
  local copies, waits for them, and re-layouts: 79.2 us -> 3.74 us
  Pallas kernels: 0 us -> 73.9 us
  waiting for transfers between devices: 71.5 us -> 0 us
  matrix products: 31.7 us -> 0 us
  starting transfers between devices: 29.4 us -> 0 us
  between operations: 14.7 us -> 0.65 us
  other arithmetic: 9.45 us -> 0 us
  loops' own time: 7.85 us -> 0 us
    all_gather x4 -> x0, blocking collectives: 193 us -> none  [the longest x1 48.6 us: prefix(): everything = lax.all_gather(value, axis)]
    unnamed x1 -> x0, blocking collectives: 124 us -> none
    pallas_call x0 -> x1, Pallas kernels: none -> 73.9 us  [per_device(): pl.pallas_call(functools.partial(body, X, Z, Y, R, KC), out_shape=(big, b...]
    all_gather x4 -> x0, waiting for transfers between devices: 54.1 us -> none  [the longest x1 54.1 us: per_device(): lax.all_gather(my_grad, 'ctx', axis=0, tiled=True)]
    unnamed x29 -> x10, local copies, waits for them, and re-layouts: 37.8 us -> 3.74 us
    dot_general x99 -> x0, matrix products: 31.7 us -> none  [the longest x25 9.52 us: block_scores(): jnp.einsum('qhd,khd->hqk', query_blk, key_blk, preferred_element_type=jnp...]
    all_to_all x8 -> x0, starting transfers between devices: 29.2 us -> none  [the longest x1 4.52 us: per_device(): lax.all_to_all(attn_output, 'head', split_axis=1, concat_axis=0, tiled=True)]
    dynamic_slice x26 -> x0, local copies, waits for them, and re-layouts: 26.9 us -> none  [the longest x25 26.8 us: one_turn(): lax.dynamic_slice_in_dim(member, offset, block_len, 0)]
  transfers between devices with their start and end apart: 12 -> 0, of which waited for: 6 -> 0; matrix products, arithmetic and copies ran while one was open for 8% -> 0% of each run, Pallas kernels for 0% -> 0%
where the time goes in v2:
time: 78.5 us; the launch traced here: 78.3 us
  Pallas kernels  73.9 us (94%)
  local copies, waits for them, and re-layouts  3.74 us (5%)
    pallas_call x1, Pallas kernels, per_device(): pl.pallas_call(functools.partial(body, X, Z, Y, R, KC), out_shape=(big, b...  73.9 us
    unnamed x10, local copies, waits for them, and re-layouts  3.74 us

profile of v2, /device:TPU:1, one launch (start us, length us, event | category | flops | bytes accessed | tf_op | source)
XLA Modules:
  0.0 78.3 jit_solution(11326249030152542653)
XLA Ops:
  0.6 73.9 %shard_map.102 = (bf16[48,1024]{1,0:T(8,128)(2,1)}, bf16[48,1024]{1,0:T(8,128)(2,1)}, bf16[48,1024]{1,0:T(8,128)(2,1)}, bf16[8,48]{1,0:T(8,128)(2,1)}) custom-call(bf16[48,1024]{1,0:T(8,128)(2,1)} %q_in.1, bf16[48,1024]{1,0:T(8,128)(2,1)} %k_in.1, bf16[48,1024]{1,0:T(8,128)(2,1)} %v_in.1, bf16[48,1024]{1,0:T(8,128)(2,1)} %g_in.1, bf16[48,1024]{1,0:T(8,128)(2,1)} %o_in.1, ...), custom_call_target="tpu_custom_call" | custom-call | tf_op jit(solution)/shard_map/pallas_call | solution.py:608
  74.6 0.0 copy-start.1
  74.6 1.6 %copy.15 = bf16[48,1024]{1,0:T(8,128)(2,1)} copy(bf16[48,1024]{1,0:T(8,128)(2,1)} %get-tuple-element.16) | data formatting | bytes 196608
  76.2 0.0 copy-done.1
  76.2 0.0 copy-start
  76.2 0.6 copy.16
  76.8 0.3 copy-done
  77.1 0.0 copy-start.2
  77.1 0.6 copy.17
  77.7 0.0 copy-done.2
  77.8 0.6 copy.18
Async XLA Ops:
  74.6 1.6 %copy-start.1 = (bf16[48,1024]{1,0:T(8,128)(2,1)S(1)}, bf16[48,1024]{1,0:T(8,128)(2,1)}, u32[]{:S(2)}) copy-start(bf16[48,1024]{1,0:T(8,128)(2,1)} %get-tuple-element.17) | copy-start | bytes 294916
  76.2 0.9 %copy-start = (bf16[48,1024]{1,0:T(8,128)(2,1)S(1)}, bf16[48,1024]{1,0:T(8,128)(2,1)}, u32[]{:S(2)}) copy-start(bf16[48,1024]{1,0:T(8,128)(2,1)} %get-tuple-element.18) | copy-start | bytes 294916
  77.1 0.7 copy-start.2

commit v3 on v2

--- a/solution.py
+++ b/solution.py
@@ -62,12 +62,12 @@
 
 
 def body(
-    X, Z, Y, R, KC,
+    X, Z, Y, R,
     q_in, k_in, v_in, g_in, o_in, gate_in, lse_in,
     dq_out, dk_out, dv_out, dgate_out,
     g_loc, o_loc, gate_pad, st_out, qst_in, kst_in,
     q_all, g_all, qst_all, k_all, v_all, kst_all, kcol, kpos, tot_all, p_all,
-    kt_all, q_row, dqt, dqt_own, row_acc, dk_acc, dv_acc, cs_acc,
+    kt_own, kt_next, kt_far, q_row, dqt, dqt_own, row_acc, dk_acc, dv_acc, cs_acc,
     sib_snd, sib_rcv, dq_snd, dq_rcv, rs_snd, rs_rcv, dk_snd, dv_snd, dk_rcv, dv_rcv, cs_snd, cs_rcv,
     after_all, dq_fin, dk_fin, dv_fin, gs_snd, gs_rcv,
     loc_sem, p1_r, p1_s, x_r, x_s, y_r, y_s, sib_r, sib_s, qs_r, qs_s, ks_r, ks_s,
@@ -131,29 +131,6 @@
         greet(dev(xr, zz, c, y))
     for dx, dc, dy in plane:
         greet(dev((x + dx) % X, z, (c + dc) % CORES, (y + dy) % Y))
-    pl.semaphore_wait(barrier, 2 * (Z - 1) + len(plane))
-
-    def columns(h_):
-        return pl.ds(pl.multiple_of(h_ * D, D), D)
-
-    z_half = z // half
-
-    def z_rows(block):
-        return pl.ds(pl.multiple_of(block * HB + (z % half) * R, R), R)
-
-    def block_rows(block):
-        return pl.ds(pl.multiple_of(block * HB, HB), HB)
-
-    for idx, src, dst in ((0, q_in, q_all), (1, g_in, g_all), (2, k_in, k_all), (3, v_in, v_all)):
-        for d in range(Z):
-            zz = (z + d) % Z
-            if idx < 2:
-                at, to, here = dst.at[2 * x + z_half, z_rows(c), :], dev(x, zz, c, y), d == 0
-            else:
-                at, to = dst.at[z_half, z_rows(y), :], dev(xk, zz, c, y)
-                here = (xk == x) if d == 0 else False
-            send(src.at[:, columns(zz)], at, p1_s.at[idx], p1_r.at[idx], to, here)
-
     for copy in loc:
         copy.wait()
     st_out[...] = jnp.zeros_like(st_out)
@@ -168,7 +145,22 @@
         st_out[h, 0:1, 0:R] = jnp.sum(product.T, axis=0, keepdims=True)
         st_out[h, 1:2, 0:R] = lse_rows[h:h + 1, :]
         st_out[h, 2:3, 0:R] = curve[h:h + 1, 0:R]
-    for d in range(Z):
+    pl.semaphore_wait(barrier, 2 * (Z - 1) + len(plane))
+
+    z_order = sorted(range(Z), key=lambda d: -min(d, Z - d))
+
+    def columns(h_):
+        return pl.ds(pl.multiple_of(h_ * D, D), D)
+
+    z_half = z // half
+
+    def z_rows(block):
+        return pl.ds(pl.multiple_of(block * HB + (z % half) * R, R), R)
+
+    def block_rows(block):
+        return pl.ds(pl.multiple_of(block * HB, HB), HB)
+
+    for d in z_order:
         zz = (z + d) % Z
         send(st_out.at[zz], qst_in.at[z], p1_s.at[4], p1_r.at[4], dev(x, zz, c, y), d == 0)
         send(
@@ -176,58 +168,73 @@
             (xk == x) if d == 0 else False,
         )
 
+    for idx, src, dst in ((0, q_in, q_all), (1, g_in, g_all), (2, k_in, k_all), (3, v_in, v_all)):
+        for d in z_order:
+            zz = (z + d) % Z
+            if idx < 2:
+                at, to, here = dst.at[x, z_half, z_rows(c), :], dev(x, zz, c, y), d == 0
+            else:
+                at, to = dst.at[z_half, z_rows(0), :], dev(xk, zz, c, y)
+                here = (xk == x) if d == 0 else False
+            send(src.at[:, columns(zz)], at, p1_s.at[idx], p1_r.at[idx], to, here)
+
     def q_block(ref, x_, c_):
-        return ref.at[pl.ds(2 * x_, 2), block_rows(c_), :]
-
-    def k_block(ref, y_):
-        return ref.at[:, block_rows(y_), :]
+        return ref.at[x_, :, block_rows(c_), :]
+
+    def k_block(ref, slot):
+        return ref.at[:, block_rows(slot), :]
 
     sibling = dev(x, z, 1 - c, y)
     queries = [functools.partial(q_block, ref, c_=c) for ref in (q_all, g_all)]
     keys = [functools.partial(k_block, ref) for ref in (k_all, v_all)]
 
-    def x_dev(x_):
-        return dev(x_, z, c, y)
-
-    def y_dev(y_):
-        return dev(x, z, c, y_)
-
-    def ring_start(blocks, arr, at, n, place, snd, rcv):
+    def x_dev(d):
+        return dev((x + d) % X, z, c, y)
+
+    def y_dev(d):
+        return dev(x, z, c, (y + d) % Y)
+
+    order = [0, 1, Y - 1, 2][:Y] if Y > 2 else [0, 1][:Y]
+
+    def q_id(d, e):
+        return (x + d) % X
+
+    def k_id(d, e):
+        return order.index((d - e) % Y)
+
+    def ring_copy(blocks, arr, name, d, e, place, section, snd, rcv):
+        src, dst = blocks[arr](name(d, 0)), blocks[arr](name(d, e))
+        return remote(src, dst, snd.at[arr, section], rcv.at[arr, section], place(e))
+
+    def ring_start(blocks, arr, name, n, place, snd, rcv):
         if n > 1:
-            block = blocks[arr](at)
-            remote(block, block, snd.at[arr, 0], rcv.at[arr, 0], place((at + 1) % n)).start()
+            ring_copy(blocks, arr, name, 0, 1, place, 0, snd, rcv).start()
         if n > 2:
-            remote(block, block, snd.at[arr, 1], rcv.at[arr, 1], place((at + n - 1) % n)).start()
-
-    def ring_onward(blocks, arr, at, n, place, snd, rcv):
+            ring_copy(blocks, arr, name, 0, -1, place, 1, snd, rcv).start()
+
+    def ring_onward(blocks, arr, name, n, place, snd, rcv):
+        came = -1 if arr == 0 else 1
+        if n > 1:
+            drain(blocks[arr](name(came, 0)), rcv.at[arr, arr if n > 2 else 0])
         if n > 2:
-            came, to = ((at + n - 1) % n, (at + 1) % n) if arr == 0 else ((at + 1) % n, (at + n - 1) % n)
-            drain(blocks[arr](came), rcv.at[arr, arr])
-            remote(blocks[arr](came), blocks[arr](came), snd.at[arr, 2], rcv.at[arr, 2], place(to)).start()
-        elif n > 1:
-            drain(blocks[arr]((at + 1) % n), rcv.at[arr, 0])
-
-    def ring_other(blocks, arr, at, n, rcv):
+            ring_copy(blocks, arr, name, came, -came, place, 2, snd, rcv).start()
+
+    def ring_other(blocks, arr, name, n, rcv):
         if n > 2:
-            drain(blocks[arr]((at + 1) % n if arr == 0 else (at + n - 1) % n), rcv.at[arr, 1 - arr])
-
-    def ring_last(blocks, arr, at, n, rcv):
+            drain(blocks[arr](name(1 if arr == 0 else -1, 0)), rcv.at[arr, 1 - arr])
+
+    def ring_last(blocks, arr, name, n, rcv):
         if n > 2:
-            drain(blocks[arr]((at + 2) % n), rcv.at[arr, 2])
-
-    def ring_sent(blocks, arr, at, n, snd):
-        block = blocks[arr](at)
+            drain(blocks[arr](name(2, 0)), rcv.at[arr, 2])
+
+    def ring_sent(blocks, arr, name, n, snd):
+        block = blocks[arr](name(0, 0))
         for k in range(0 if n == 1 else 1 if n == 2 else 3):
             drain(block, snd.at[arr, k])
 
     def to_sibling(arr, x_):
         block = queries[arr](x_)
         remote(block, block, sib_s.at[arr, x_], sib_r.at[arr, x_], sibling).start()
-
-    for arr in range(2):
-        drain(queries[arr](x), p1_r.at[arr])
-        ring_start(queries, arr, x, X, x_dev, x_s, x_r)
-        to_sibling(arr, x)
 
     def wide(tile):
         return jnp.concatenate([tile, jnp.zeros((8, B - 128), F32)], axis=1) if B > 128 else tile[:, :B]
@@ -266,37 +273,29 @@
     kst_all[y] = assemble(kst_in)
     for dy in range(1, Y):
         mine = kst_all.at[y]
-        remote(mine, mine, ks_s.at[0], ks_r.at[0], y_dev((y + dy) % Y)).start()
+        remote(mine, mine, ks_s.at[0], ks_r.at[0], y_dev(dy)).start()
     for arr in range(2):
-        drain(keys[arr](y), p1_r.at[2 + arr])
-        ring_start(keys, arr, y, Y, y_dev, y_s, y_r)
+        drain(queries[arr](x), p1_r.at[arr])
+        ring_start(queries, arr, q_id, X, x_dev, x_s, x_r)
+        to_sibling(arr, x)
 
     dk_acc[...] = jnp.zeros_like(dk_acc)
     dv_acc[...] = jnp.zeros_like(dv_acc)
     cs_acc[...] = jnp.zeros_like(cs_acc)
     dqt[...] = jnp.zeros_like(dqt)
     row_acc[...] = jnp.zeros_like(row_acc)
-    k_at = iota((Y * HB, 128), 0)
-    k_y = section_of(k_at, HB, Y)
-    k_rest = k_at - HB * k_y
-    k_z = section_of(k_rest, R, half)
-    kpos[...] = k_z * (CY * R) + c * (Y * R) + k_y * R + (k_rest - R * k_z)
-    q_at = iota((8, B), 1)
-    q_c = section_of(q_at, HB, CORES)
-    q_rest = q_at - HB * q_c
+    k_at = iota((HB, 128), 0)
+    k_z = section_of(k_at, R, half)
+    for slot, dy in enumerate(order):
+        k_y = (y + dy) % Y
+        kpos[slot * HB:(slot + 1) * HB, :] = k_z * (CY * R) + c * (Y * R) + k_y * R + (k_at - R * k_z)
+    q_at = iota((8, 2 * B), 1)
+    q_half = (q_at >= B).astype(jnp.int32)
+    q_rest = q_at - B * q_half
+    q_c = section_of(q_rest, HB, CORES)
+    q_rest = q_rest - HB * q_c
     q_z = section_of(q_rest, R, half)
-    qpos = q_z * (CY * R) + q_c * (Y * R) + y * R + (q_rest - R * q_z)
-
-    for arr in range(2):
-        ring_onward(queries, arr, x, X, x_dev, x_s, x_r)
-        if X > 1:
-            to_sibling(arr, (x + X - 1) % X if arr == 0 or X == 2 else (x + 1) % X)
-    for arr in range(2):
-        ring_onward(keys, arr, y, Y, y_dev, y_s, y_r)
-    if X > 2:
-        for arr in range(2):
-            ring_other(queries, arr, x, X, x_r)
-            to_sibling(arr, (x + 1) % X if arr == 0 else (x + X - 1) % X)
+    qpos = (q_half * half + q_z) * (CY * R) + q_c * (Y * R) + y * R + (q_rest - R * q_z)
 
     few = X * CY - 1
     drain(tot_all.at[pl.ds(0, few)], t_r.at[0])
@@ -332,119 +331,185 @@
             bias = along_lanes(p_all[x_ * CY + c_ * Y + y])
             stat = qst_all[x_ * CORES + c_]
             rows.append(jnp.where(iota((8, B), 0) == 0, (stat + bias) * LOG2E, stat))
-        lo, hi = halves(*rows)
-        q_row[2 * x_] = lo
-        q_row[2 * x_ + 1] = hi
+        q_row[x_] = jnp.concatenate(halves(*rows), axis=1)
 
     if Y > 1:
         drain(kst_all.at[pl.ds(0, Y - 1)], ks_r.at[0])
-    for y_ in range(Y):
+    for slot, dy in enumerate(order):
+        y_ = (y + dy) % Y
         tile = jnp.where(row_at < half, p_all[x * CY + c * Y + y_], p_all[xr * CY + c * Y + y_])
         column = ((kst_all[y_] + along_lanes(tile)) * LOG2E).T[:, 2:3]
         spread_column = jnp.broadcast_to(column, (B, 128))
-        kcol[0, y_ * HB:(y_ + 1) * HB, :] = spread_column[0:HB]
-        kcol[1, y_ * HB:(y_ + 1) * HB, :] = spread_column[HB:B]
+        kcol[0, slot * HB:(slot + 1) * HB, :] = spread_column[0:HB]
+        kcol[1, slot * HB:(slot + 1) * HB, :] = spread_column[HB:B]
+
+    def pair(x_, kh, rows, turned, masked):
+        q_blk, g_blk = q_all[x_].reshape(2 * B, D), g_all[x_].reshape(2 * B, D)
+        stat = q_row[x_]
+        row, delta = stat[0:1], stat[1:2]
+        k_blk, v_blk = k_all[kh, rows, :], v_all[kh, rows, :]
+        s = dot(k_blk, q_blk, NT)
+        prob = jnp.exp2(s * (scale * LOG2E) + row - lanes(kcol[kh, rows, :], 2 * B))
+        if masked:
+            at = kpos[rows, :] + kh * (half * CY * R)
+            prob = jnp.where(lanes(at, 2 * B) <= qpos[0:1], prob, 0.0)
+        grad = prob * (dot(v_blk, g_blk, NT) - delta)
+        prob_half, grad_half = prob.astype(BF16), grad.astype(BF16)
+        dv_acc[kh, rows, :] += dot(prob_half, g_blk, NN)
+        dk_acc[kh, rows, :] += dot(grad_half, q_blk, NN)
+        dqt[x_] += dot(turned[kh], grad_half, NN)
+        row_acc[x_, 0:1, :] += jnp.sum(grad, axis=0, keepdims=True)
+        if B > 64:
+            folded = grad[:, 0:128]
+            for lane in range(128, 2 * B, 128):
+                folded = folded + grad[:, lane:lane + 128]
+            cs_acc[kh, rows, :] += folded
+        else:
+            cs_acc[kh, rows, 0:2 * B] += grad
+
+    def key_turn(turned, rows):
+        for kh in range(2):
+            turned[kh] = k_all[kh, rows, :].astype(F32).T.astype(BF16)
+
+    kt_all = (kt_own, kt_next, kt_far) if Y > 2 else (kt_own, kt_far)
+
+    def sib_wait(x_):
+        for arr in range(2):
+            drain(q_block((q_all, g_all)[arr], x_, 1 - c), sib_r.at[arr, x_])
+
+    def curve_send(slot):
+        rows, dy = pl.ds(slot * HB, HB), order[slot]
+        column = jnp.concatenate([cs_acc[0, rows, :], cs_acc[1, rows, :]], axis=0)
+        cs_snd[slot] = jnp.broadcast_to(jnp.sum(column.T, axis=0, keepdims=True), (8, B))
+        send(cs_snd.at[slot], cs_rcv.at[0, y], cs_s.at[0], cs_r.at[0], y_dev(dy), dy == 0)
+        send(cs_snd.at[slot], cs_rcv.at[1, y], cs_s.at[1], cs_r.at[1], dev(xr, z, c, (y + dy) % Y), False)
+
+    key_sums = ((dk_acc, dk_snd, dk_rcv, scale), (dv_acc, dv_snd, dv_rcv, 1.0))
+
+    def key_send(slot):
+        side = order.index(-order[slot] % Y) - 1
+        for arr, (acc, snd, rcv, factor) in enumerate(key_sums):
+            for kh in range(2):
+                snd[slot, kh] = (acc[kh, slot * HB:(slot + 1) * HB, :] * factor).astype(BF16)
+            remote(
+                snd.at[slot], rcv.at[side], dk_s.at[arr, slot], dk_r.at[arr, side], y_dev(order[slot])
+            ).start()
+
+    def query_steps(i):
+        if i == 1:
+            for arr in range(2):
+                ring_onward(queries, arr, q_id, X, x_dev, x_s, x_r)
+                to_sibling(arr, (x + X - 1) % X if arr == 0 else (x + 1) % X)
+            if X > 2:
+                for arr in range(2):
+                    ring_other(queries, arr, q_id, X, x_r)
+                    to_sibling(arr, (x + 1) % X if arr == 0 else (x + X - 1) % X)
+        if i == X - 1:
+            for arr in range(2):
+                ring_onward(keys, arr, k_id, Y, y_dev, y_s, y_r)
+        if i == 3:
+            for arr in range(2):
+                ring_last(queries, arr, q_id, X, x_r)
+                to_sibling(arr, (x + 2) % X)
+        if i:
+            sib_wait((x + x_order[i]) % X)
+
+    def rows_done(x_):
+        tiles = halves(row_acc[x_, :, 0:B], row_acc[x_, :, B:2 * B])
+        for c_ in range(CORES):
+            rs_snd[x_ * CORES + c_] = tiles[c_]
+            src, dst = rs_snd.at[x_ * CORES + c_], rs_rcv.at[xc]
+            here = jnp.logical_and(x_ == x, c_ == c)
+            send(src, dst, rs_s.at[0], rs_r.at[0], dev(x_, z, c_, y), here)
+        dq_part = dqt[x_].T * scale
+        for hf in range(2):
+            lower, upper = dq_part[hf * B:hf * B + HB], dq_part[hf * B + HB:hf * B + B]
+            dqt_own[x_, hf] = jnp.where(c == 0, lower, upper)
+            sib_snd[x_, hf] = jnp.where(c == 0, upper, lower).astype(BF16)
+        remote(sib_snd.at[x_], sib_rcv.at[x_], dsib_s.at[x_], dsib_r.at[x_], sibling).start()
+
+    def rows_home(x_):
+        drain(sib_rcv.at[x_], dsib_r.at[x_])
+        dq_snd[x_] = (dqt_own[x_] + sib_rcv[x_].astype(F32)).astype(BF16)
+        remote(dq_snd.at[x_], dq_rcv.at[x], dq_s.at[x_], dq_r.at[x], dev(x_, z, c, y)).start()
+
+    x_order = [0, 1, X - 1, 2][:X] if X > 2 else [0, 1][:X]
+    bands = {1: [(0, 1)], 2: [(0, 1), (1, 1)], 4: [(0, 1), (1, 2), (3, 1)]}[Y]
+
+    def pick(values, at):
+        return sum(jnp.where(at == k, v, 0) for k, v in enumerate(values))
 
     for arr in range(2):
-        ring_other(keys, arr, y, Y, y_r)
-    for arr in range(2):
-        ring_last(keys, arr, y, Y, y_r)
-    if X > 2:
-        for arr in range(2):
-            ring_last(queries, arr, x, X, x_r)
-            to_sibling(arr, (x + 2) % X)
-    for arr in range(2):
-        for x_ in range(X):
-            drain(q_block(q_all, x_, 1 - c), sib_r.at[arr, x_])
-
-    def pair(u, kh, masked):
-        q_blk, g_blk, stat = q_all[u], g_all[u], q_row[u]
-        row, delta = stat[0:1], stat[1:2]
-
-        def chunk(k, carry):
-            at = pl.ds(pl.multiple_of(k * KC, KC), KC)
-            k_blk, v_blk = k_all[kh, at, :], v_all[kh, at, :]
-            s = dot(k_blk, q_blk, NT)
-            prob = jnp.exp2(s * (scale * LOG2E) + row - lanes(kcol[kh, at, :], B))
-            if masked:
-                prob = jnp.where(lanes(kpos[at, :], B) <= qpos[0:1], prob, 0.0)
-            grad = prob * (dot(v_blk, g_blk, NT) - delta)
-            prob_half, grad_half = prob.astype(BF16), grad.astype(BF16)
-            dv_acc[kh, at, :] += dot(prob_half, g_blk, NN)
-            dk_acc[kh, at, :] += dot(grad_half, q_blk, NN)
-            dqt[u] += dot(kt_all[kh, k], grad_half, NN)
-            row_acc[u, 0:1, :] += jnp.sum(grad, axis=0, keepdims=True)
-            if B > 128:
-                folded = grad[:, 0:128]
-                for lane in range(128, B, 128):
-                    folded = folded + grad[:, lane:lane + 128]
-                cs_acc[kh, at, :] += folded
-            else:
-                cs_acc[kh, at, 0:B] += grad
+        drain(keys[arr](0), p1_r.at[2 + arr])
+        ring_start(keys, arr, k_id, Y, y_dev, y_s, y_r)
+    sib_wait(x)
+
+    def band(first_slot, slots, turned, last, before_step):
+        rows = pl.ds(first_slot * HB, slots * HB)
+        key_turn(turned, rows)
+
+        def step(i, carry):
+            for k in range(1, X):
+                if before_step:
+                    pl.when(i == k)(functools.partial(before_step, k))
+            x_ = (x + pick(x_order, X - 1 - i if last else i)) % X
+
+            def key_half(kh, inner):
+                first = jnp.where(kh == 0, x, xr)
+
+                @pl.when(x_ > first)
+                def _():
+                    pair(x_, kh, rows, turned, False)
+
+                @pl.when(x_ == first)
+                def _():
+                    pair(x_, kh, rows, turned, True)
+
+                return inner
+
+            lax.fori_loop(0, 2, key_half, 0)
+            if last:
+                rows_done(x_)
+
+                @pl.when(i > 0)
+                def _():
+                    rows_home((x + pick(x_order, X - i)) % X)
+
             return carry
 
-        lax.fori_loop(0, Y * HB // KC, chunk, 0)
-
-    for kh in range(2):
-        for k in range(Y * HB // KC):
-            kt_all[kh, k] = k_all[kh, k * KC:(k + 1) * KC, :].astype(F32).T.astype(BF16)
-    for kh in range(2):
-        first = 2 * x if kh == 0 else 2 * xr + 1
-        pair(first, kh, True)
-
-        def one(u, carry, kh=kh):
-            pair(u, kh, False)
-            return carry
-
-        lax.fori_loop(first + 1, 2 * X, one, 0)
-
-    for x_ in range(X):
-        lo, hi = halves(row_acc[2 * x_], row_acc[2 * x_ + 1])
-        for c_, tile in ((0, lo), (1, hi)):
-            rs_snd[x_ * CORES + c_] = tile
-
-    def team(dx, dc):
-        return (x + dx) % X, (c + dc) % CORES
-
-    for dx, dc in [(0, 0)] + q_team:
-        x_, c_ = team(dx, dc)
-        send(
-            rs_snd.at[x_ * CORES + c_], rs_rcv.at[xc], rs_s.at[0], rs_r.at[0], dev(x_, z, c_, y), (dx, dc) == (0, 0)
-        )
-    for y_ in range(Y):
-        rows = pl.ds(y_ * HB, HB)
-        column = jnp.concatenate([cs_acc[0, rows, :], cs_acc[1, rows, :]], axis=0)
-        cs_snd[y_] = jnp.broadcast_to(jnp.sum(column.T, axis=0, keepdims=True), (8, B))
-    for dy in range(Y):
-        y_ = (y + dy) % Y
-        send(cs_snd.at[y_], cs_rcv.at[0, y], cs_s.at[0], cs_r.at[0], y_dev(y_), dy == 0)
-        send(cs_snd.at[y_], cs_rcv.at[1, y], cs_s.at[1], cs_r.at[1], dev(xr, z, c, y_), False)
-
-    for dx in range(X):
-        x_ = (x + dx) % X
-        for hf in range(2):
-            dqt_unit = dqt[2 * x_ + hf].T * scale
-            lower, upper = dqt_unit[0:HB], dqt_unit[HB:B]
-            mine = jnp.where(c == 0, lower, upper)
-            theirs = jnp.where(c == 0, upper, lower)
-            sib_snd[x_, hf] = theirs.astype(BF16)
-            dqt_own[x_, hf] = mine
-        remote(sib_snd.at[x_], sib_rcv.at[x_], dsib_s.at[x_], dsib_r.at[x_], sibling).start()
-
-    for dy in range(1, Y):
-        y_ = (y + dy) % Y
-        rows = block_rows(y_)
-        for kh in range(2):
-            dk_snd[y_, kh] = (dk_acc[kh, rows, :] * scale).astype(BF16)
-            dv_snd[y_, kh] = dv_acc[kh, rows, :].astype(BF16)
-        remote(dk_snd.at[y_], dk_rcv.at[y], dk_s.at[0, y_], dk_r.at[0, y], y_dev(y_)).start()
-        remote(dv_snd.at[y_], dv_rcv.at[y], dk_s.at[1, y_], dk_r.at[1, y], y_dev(y_)).start()
-
+        lax.fori_loop(0, X, step, 0)
+
+    for b, (first_slot, slots) in enumerate(bands):
+        if b == 1:
+            for arr in range(2):
+                ring_other(keys, arr, k_id, Y, y_r)
+        if b == 2:
+            for arr in range(2):
+                ring_last(keys, arr, k_id, Y, y_r)
+        band(first_slot, slots, kt_all[b], b == len(bands) - 1, None if b else query_steps)
+        for slot in range(first_slot, first_slot + slots):
+            curve_send(slot)
+        if b:
+            for slot in range(first_slot, first_slot + slots):
+                key_send(slot)
+
+    def give_back(fin, out, idx, keyed):
+        for d in z_order:
+            zz = (z + d) % Z
+            src = fin.at[zz // half, pl.ds(pl.multiple_of((zz % half) * R, R), R), :]
+            dst = out.at[:, columns(z)]
+            at_x = jnp.where(zz < half, x, xr) if keyed else x
+            here = False if d else ((at_x == x) if keyed else True)
+            send(src, dst, f_s.at[idx], f_r.at[idx], dev(at_x, zz, c, y), here)
+
+    drain(sib_rcv.at[x], dsib_r.at[x])
+    dq_sum = dqt_own[x] + sib_rcv[x].astype(F32)
     for dx in range(1, X):
         x_ = (x + dx) % X
-        drain(sib_rcv.at[x_], dsib_r.at[x_])
-        dq_snd[x_] = (dqt_own[x_] + sib_rcv[x_].astype(F32)).astype(BF16)
-        remote(dq_snd.at[x_], dq_rcv.at[x], dq_s.at[x_], dq_r.at[x], x_dev(x_)).start()
+        drain(dq_rcv.at[x_], dq_r.at[x_])
+        dq_sum = dq_sum + dq_rcv[x_].astype(F32)
+    dq_fin[...] = dq_sum.astype(BF16)
+    give_back(dq_fin, dq_out, 0, False)
 
     drain(rs_rcv, rs_r.at[0])
     drain(cs_rcv.at[0], cs_r.at[0])
@@ -463,36 +528,16 @@
     after_all[x * CY + cy] = totals
     spread(after_all, x * CY + cy, t_r.at[1], t_s.at[1])
 
-    def give_back(fin, out, idx, keyed):
-        for d in range(Z):
-            zz = (z + d) % Z
-            src = fin.at[zz // half, pl.ds(pl.multiple_of((zz % half) * R, R), R), :]
-            dst = out.at[:, columns(z)]
-            at_x = jnp.where(zz < half, x, xr) if keyed else x
-            here = False if d else ((at_x == x) if keyed else True)
-            send(src, dst, f_s.at[idx], f_r.at[idx], dev(at_x, zz, c, y), here)
-
     for rcv, acc, fin, out, idx, factor in (
         (dk_rcv, dk_acc, dk_fin, dk_out, 1, scale), (dv_rcv, dv_acc, dv_fin, dv_out, 2, 1.0)
     ):
-        own = block_rows(y)
-        sums = [acc[kh, own, :] * factor for kh in range(2)]
-        for dy in range(1, Y):
-            y_ = (y + dy) % Y
-            drain(rcv.at[y_], dk_r.at[idx - 1, y_])
-            sums = [sums[kh] + rcv[y_, kh].astype(F32) for kh in range(2)]
+        sums = [acc[kh, 0:HB, :] * factor for kh in range(2)]
+        for side in range(Y - 1):
+            drain(rcv.at[side], dk_r.at[idx - 1, side])
+            sums = [sums[kh] + rcv[side, kh].astype(F32) for kh in range(2)]
         for kh in range(2):
             fin[kh] = sums[kh].astype(BF16)
         give_back(fin, out, idx, True)
-
-    drain(sib_rcv.at[x], dsib_r.at[x])
-    dq_sum = dqt_own[x] + sib_rcv[x].astype(F32)
-    for dx in range(1, X):
-        x_ = (x + dx) % X
-        drain(dq_rcv.at[x_], dq_r.at[x_])
-        dq_sum = dq_sum + dq_rcv[x_].astype(F32)
-    dq_fin[...] = dq_sum.astype(BF16)
-    give_back(dq_fin, dq_out, 0, False)
 
     drain(after_all.at[pl.ds(0, few)], t_r.at[1])
     after = jnp.zeros((8, 128), F32)
@@ -508,7 +553,7 @@
     for s in range(Z):
         moved = pltpu.roll(gate_sum, (B - s * R) % B, 1) if s else gate_sum
         gs_snd[s] = moved[:, 0:128] if B >= 128 else jnp.concatenate([moved, jnp.zeros((8, 128 - B), F32)], axis=1)
-    for d in range(Z):
+    for d in z_order:
         zz = (z + d) % Z
         send(gs_snd.at[zz], gs_rcv.at[z], f_s.at[3], f_r.at[3], dev(x, zz, c, y), d == 0)
     drain(gs_rcv, f_r.at[3])
@@ -518,13 +563,12 @@
     dgate_out[...] = (by_head[0:H, 0:R] * jax.nn.sigmoid(-gate_float)).astype(BF16)
 
     for arr in range(2):
-        ring_sent(queries, arr, x, X, x_s)
-        ring_sent(keys, arr, y, Y, y_s)
+        ring_sent(queries, arr, q_id, X, x_s)
+        ring_sent(keys, arr, k_id, Y, y_s)
         for x_ in range(X):
             drain(queries[arr](x_), sib_s.at[arr, x_])
-        for dy in range(1, Y):
-            y_ = (y + dy) % Y
-            drain(dk_snd.at[y_], dk_s.at[arr, y_])
+        for slot in range(1, Y):
+            drain(dk_snd.at[slot], dk_s.at[arr, slot])
     drain(qst_all.at[pl.ds(0, len(q_team))], qs_s.at[0])
     drain(rs_snd.at[pl.ds(0, len(q_team))], rs_s.at[0])
     if Y > 1:
@@ -576,12 +620,11 @@
     R, columns = args[0].shape
     D, Z, C = WIDTH, columns // WIDTH, CORES
     HB, B, H = Z // 2 * R, Z * R, Z
-    KC = min(256, Y * HB)
     vm = pltpu.VMEM
     dma = pltpu.SemaphoreType.DMA
     any_spec = pl.BlockSpec(memory_space=pl.ANY)
     vm_spec = pl.BlockSpec(memory_space=pltpu.VMEM)
-    queries, keys = (2 * X, C * HB, D), (2, Y * HB, D)
+    queries, keys = (X, 2, C * HB, D), (2, Y * HB, D)
     block, tile = (2, HB, D), (8, 128)
     scratch = [
         vm((R, columns), BF16), vm((R, columns), BF16), vm(tile, F32),
@@ -590,8 +633,8 @@
         vm(keys, BF16), vm(keys, BF16), vm((Y, 8, B), F32),
         vm((2, Y * HB, 128), F32), vm((Y * HB, 128), jnp.int32),
         vm((X * C * Y,) + tile, F32), vm((X * C * Y,) + tile, F32),
-        vm((2, Y * HB // KC, D, KC), BF16), vm((2 * X, 8, B), F32),
-        vm((2 * X, D, B), F32), vm((X,) + block, F32), vm((2 * X, 8, B), F32),
+        vm((2, D, HB), BF16), vm((2, D, 2 * HB), BF16), vm((2, D, HB), BF16), vm((X, 8, 2 * B), F32),
+        vm((X, D, 2 * B), F32), vm((X,) + block, F32), vm((X, 8, 2 * B), F32),
         vm(keys, F32), vm(keys, F32), vm((2, Y * HB, 128), F32),
         vm((X,) + block, BF16), vm((X,) + block, BF16), vm((X,) + block, BF16), vm((X,) + block, BF16),
         vm((X * C, 8, B), F32), vm((X * C, 8, B), F32),
@@ -606,7 +649,7 @@
     ]
     big = jax.ShapeDtypeStruct((R, columns), BF16)
     dq, dk, dv, dgate = pl.pallas_call(
-        functools.partial(body, X, Z, Y, R, KC),
+        functools.partial(body, X, Z, Y, R),
         out_shape=(big, big, big, jax.ShapeDtypeStruct((H, R), BF16)),
         in_specs=[any_spec] * 5 + [vm_spec] * 2,
         out_specs=(any_spec, any_spec, any_spec, vm_spec),

time: 78.5 us -> 65.3 us (0.83)
  Pallas kernels: 73.9 us -> 60.6 us
    pallas_call x1, Pallas kernels: 73.9 us -> 60.6 us  [per_device(): pl.pallas_call(functools.partial(body, X, Z, Y, R), out_shape=(big, big,...]
where the time goes in v3:
time: 65.3 us; the launch traced here: 65 us
  Pallas kernels  60.6 us (93%)
  local copies, waits for them, and re-layouts  3.74 us (6%)
    pallas_call x1, Pallas kernels, per_device(): pl.pallas_call(functools.partial(body, X, Z, Y, R), out_shape=(big, big,...  60.6 us
    unnamed x10, local copies, waits for them, and re-layouts  3.74 us

profile of v3, /device:TPU:1, one launch (start us, length us, event | category | flops | bytes accessed | tf_op | source)
XLA Modules:
  0.0 65.0 jit_solution(16433048007567185229)
XLA Ops:
  0.6 60.6 %shard_map.102 = (bf16[48,1024]{1,0:T(8,128)(2,1)}, bf16[48,1024]{1,0:T(8,128)(2,1)}, bf16[48,1024]{1,0:T(8,128)(2,1)}, bf16[8,48]{1,0:T(8,128)(2,1)}) custom-call(bf16[48,1024]{1,0:T(8,128)(2,1)} %q_in.1, bf16[48,1024]{1,0:T(8,128)(2,1)} %k_in.1, bf16[48,1024]{1,0:T(8,128)(2,1)} %v_in.1, bf16[48,1024]{1,0:T(8,128)(2,1)} %g_in.1, bf16[48,1024]{1,0:T(8,128)(2,1)} %o_in.1, ...), custom_call_target="tpu_custom_call" | custom-call | tf_op jit(solution)/shard_map/pallas_call | solution.py:651
  61.3 0.0 copy-start.1
  61.3 1.6 %copy.15 = bf16[48,1024]{1,0:T(8,128)(2,1)} copy(bf16[48,1024]{1,0:T(8,128)(2,1)} %get-tuple-element.16) | data formatting | bytes 196608
  62.9 0.0 copy-done.1
  62.9 0.0 copy-start
  62.9 0.6 copy.16
  63.5 0.3 copy-done
  63.8 0.0 copy-start.2
  63.8 0.6 copy.17
  64.4 0.0 copy-done.2
  64.5 0.6 copy.18
Async XLA Ops:
  61.3 1.6 %copy-start.1 = (bf16[48,1024]{1,0:T(8,128)(2,1)S(1)}, bf16[48,1024]{1,0:T(8,128)(2,1)}, u32[]{:S(2)}) copy-start(bf16[48,1024]{1,0:T(8,128)(2,1)} %get-tuple-element.17) | copy-start | bytes 294916
  62.9 0.9 %copy-start = (bf16[48,1024]{1,0:T(8,128)(2,1)S(1)}, bf16[48,1024]{1,0:T(8,128)(2,1)}, u32[]{:S(2)}) copy-start(bf16[48,1024]{1,0:T(8,128)(2,1)} %get-tuple-element.18) | copy-start | bytes 294916
  63.8 0.7 %copy-start.2 = (bf16[8,48]{1,0:T(8,128)(2,1)S(1)}, bf16[8,48]{1,0:T(8,128)(2,1)}, u32[]{:S(2)}) copy-start(bf16[8,48]{1,0:T(8,128)(2,1)} %get-tuple-element.11) | copy-start | bytes 2308

commit v4 on v3

--- a/solution.py
+++ b/solution.py
@@ -65,11 +65,11 @@
     X, Z, Y, R,
     q_in, k_in, v_in, g_in, o_in, gate_in, lse_in,
     dq_out, dk_out, dv_out, dgate_out,
-    g_loc, o_loc, gate_pad, st_out, qst_in, kst_in,
+    g_loc, o_loc, gate_pad, st_q, st_k, qst_in, kst_in,
     q_all, g_all, qst_all, k_all, v_all, kst_all, kcol, kpos, tot_all, p_all,
     kt_own, kt_next, kt_far, q_row, dqt, dqt_own, row_acc, dk_acc, dv_acc, cs_acc,
     sib_snd, sib_rcv, dq_snd, dq_rcv, rs_snd, rs_rcv, dk_snd, dv_snd, dk_rcv, dv_rcv, cs_snd, cs_rcv,
-    after_all, dq_fin, dk_fin, dv_fin, gs_snd, gs_rcv,
+    after_own, after_all, dq_fin, dk_fin, dv_fin, gs_snd, gs_rcv,
     loc_sem, p1_r, p1_s, x_r, x_s, y_r, y_s, sib_r, sib_s, qs_r, qs_s, ks_r, ks_s,
     t_r, t_s, dsib_r, dsib_s, dq_r, dq_s, rs_r, rs_s, dk_r, dk_s, cs_r, cs_s, f_r, f_s,
 ):
@@ -133,7 +133,8 @@
         greet(dev((x + dx) % X, z, (c + dc) % CORES, (y + dy) % Y))
     for copy in loc:
         copy.wait()
-    st_out[...] = jnp.zeros_like(st_out)
+    st_q[...] = jnp.zeros_like(st_q)
+    st_k[...] = jnp.zeros_like(st_k)
     gate_pad[...] = jnp.zeros_like(gate_pad)
     gate_float = gate_in[...].astype(F32)
     gate_pad[0:H, 0:R] = jax.nn.log_sigmoid(gate_float)
@@ -142,9 +143,10 @@
     for h in range(H):
         cut = slice(h * D, (h + 1) * D)
         product = g_loc[:, cut].astype(F32) * o_loc[:, cut].astype(F32)
-        st_out[h, 0:1, 0:R] = jnp.sum(product.T, axis=0, keepdims=True)
-        st_out[h, 1:2, 0:R] = lse_rows[h:h + 1, :]
-        st_out[h, 2:3, 0:R] = curve[h:h + 1, 0:R]
+        st_q[h, 0:1, 0:R] = curve[h:h + 1, 0:R] - lse_rows[h:h + 1, :]
+        st_q[h, 0:1, 127:128] = curve[h:h + 1, R - 1:R]
+        st_q[h, 1:2, 0:R] = jnp.sum(product.T, axis=0, keepdims=True)
+        st_k[h, 0:1, 0:R] = curve[h:h + 1, 0:R]
     pl.semaphore_wait(barrier, 2 * (Z - 1) + len(plane))
 
     z_order = sorted(range(Z), key=lambda d: -min(d, Z - d))
@@ -162,9 +164,9 @@
 
     for d in z_order:
         zz = (z + d) % Z
-        send(st_out.at[zz], qst_in.at[z], p1_s.at[4], p1_r.at[4], dev(x, zz, c, y), d == 0)
+        send(st_q.at[zz], qst_in.at[z], p1_s.at[4], p1_r.at[4], dev(x, zz, c, y), d == 0)
         send(
-            st_out.at[zz], kst_in.at[z], p1_s.at[5], p1_r.at[5], dev(xk, zz, c, y),
+            st_k.at[zz], kst_in.at[z], p1_s.at[5], p1_r.at[5], dev(xk, zz, c, y),
             (xk == x) if d == 0 else False,
         )
 
@@ -239,17 +241,20 @@
     def wide(tile):
         return jnp.concatenate([tile, jnp.zeros((8, B - 128), F32)], axis=1) if B > 128 else tile[:, :B]
 
-    def assemble(ref):
-        total = wide(ref[0])
-        for s in range(1, Z):
-            total = total + pltpu.roll(wide(ref[s]), s * R, 1)
+    in_piece_lanes = iota((8, 128), 1) < R
+
+    def assemble(ref, at):
+        total = jnp.zeros((8, B), F32)
+        for s in range(Z):
+            tile = jnp.where(in_piece_lanes, jnp.broadcast_to(ref[s, at:at + 1, :], (8, 128)), 0.0)
+            total = total + (pltpu.roll(wide(tile), s * R, 1) if s else wide(tile))
         return total
 
     row_at = iota((8, 128), 0)
     drain(qst_in, p1_r.at[4])
     totals = jnp.zeros((8, 128), F32)
     for s in range(Z):
-        totals = jnp.where(row_at == s, jnp.broadcast_to(qst_in[s, 2:3, R - 1:R], (8, 128)), totals)
+        totals = jnp.where(row_at == s, jnp.broadcast_to(qst_in[s, 0:1, 127:128], (8, 128)), totals)
     tot_all[x * CY + cy] = totals
 
     def spread(ref, slot, semr, sems):
@@ -258,11 +263,9 @@
             remote(ref.at[slot], ref.at[slot], sems, semr, to).start()
 
     spread(tot_all, x * CY + cy, t_r.at[0], t_s.at[0])
-    q_stats = assemble(qst_in)
     xc = x * CORES + c
-    qst_all[xc, 0:1, :] = q_stats[2:3] - q_stats[1:2]
-    qst_all[xc, 1:2, :] = q_stats[0:1]
-    qst_all[xc, 2:8, :] = jnp.zeros((6, B), F32)
+    for at in range(2):
+        qst_all[xc, at:at + 1, :] = assemble(qst_in, at)[0:1]
     q_team = [(dx, dc) for dx in range(X) for dc in range(CORES)][1:]
     for dx, dc in q_team:
         x_, c_ = (x + dx) % X, (c + dc) % CORES
@@ -270,7 +273,7 @@
         remote(mine, mine, qs_s.at[0], qs_r.at[0], dev(x_, z, c_, y)).start()
 
     drain(kst_in, p1_r.at[5])
-    kst_all[y] = assemble(kst_in)
+    kst_all[y] = assemble(kst_in, 0)[0:1]
     for dy in range(1, Y):
         mine = kst_all.at[y]
         remote(mine, mine, ks_s.at[0], ks_r.at[0], y_dev(dy)).start()
@@ -284,6 +287,7 @@
     cs_acc[...] = jnp.zeros_like(cs_acc)
     dqt[...] = jnp.zeros_like(dqt)
     row_acc[...] = jnp.zeros_like(row_acc)
+    after_own[...] = jnp.zeros((8, 128), F32)
     k_at = iota((HB, 128), 0)
     k_z = section_of(k_at, R, half)
     for slot, dy in enumerate(order):
@@ -330,7 +334,7 @@
         for c_ in range(CORES):
             bias = along_lanes(p_all[x_ * CY + c_ * Y + y])
             stat = qst_all[x_ * CORES + c_]
-            rows.append(jnp.where(iota((8, B), 0) == 0, (stat + bias) * LOG2E, stat))
+            rows.append(jnp.where(iota((8, B), 0) == 0, (stat[0:1] + bias) * LOG2E, jnp.broadcast_to(stat[1:2], (8, B))))
         q_row[x_] = jnp.concatenate(halves(*rows), axis=1)
 
     if Y > 1:
@@ -338,34 +342,38 @@
     for slot, dy in enumerate(order):
         y_ = (y + dy) % Y
         tile = jnp.where(row_at < half, p_all[x * CY + c * Y + y_], p_all[xr * CY + c * Y + y_])
-        column = ((kst_all[y_] + along_lanes(tile)) * LOG2E).T[:, 2:3]
+        column = jnp.broadcast_to((kst_all[y_] + along_lanes(tile)) * LOG2E, (8, B)).T[:, 0:1]
         spread_column = jnp.broadcast_to(column, (B, 128))
         kcol[0, slot * HB:(slot + 1) * HB, :] = spread_column[0:HB]
         kcol[1, slot * HB:(slot + 1) * HB, :] = spread_column[HB:B]
 
-    def pair(x_, kh, rows, turned, masked):
-        q_blk, g_blk = q_all[x_].reshape(2 * B, D), g_all[x_].reshape(2 * B, D)
-        stat = q_row[x_]
-        row, delta = stat[0:1], stat[1:2]
+    def pair(x_, kh, rows, turned, first_lane, masked):
+        count = 2 * B - first_lane
+        part = slice(first_lane, 2 * B)
+        if first_lane:
+            q_blk, g_blk = q_all[x_, 1], g_all[x_, 1]
+        else:
+            q_blk, g_blk = q_all[x_].reshape(2 * B, D), g_all[x_].reshape(2 * B, D)
+        row, delta = q_row[x_, 0:1, part], q_row[x_, 1:2, part]
         k_blk, v_blk = k_all[kh, rows, :], v_all[kh, rows, :]
         s = dot(k_blk, q_blk, NT)
-        prob = jnp.exp2(s * (scale * LOG2E) + row - lanes(kcol[kh, rows, :], 2 * B))
+        prob = jnp.exp2(s * (scale * LOG2E) + row - lanes(kcol[kh, rows, :], count))
         if masked:
             at = kpos[rows, :] + kh * (half * CY * R)
-            prob = jnp.where(lanes(at, 2 * B) <= qpos[0:1], prob, 0.0)
+            prob = jnp.where(lanes(at, count) <= qpos[0:1, part], prob, 0.0)
         grad = prob * (dot(v_blk, g_blk, NT) - delta)
         prob_half, grad_half = prob.astype(BF16), grad.astype(BF16)
         dv_acc[kh, rows, :] += dot(prob_half, g_blk, NN)
         dk_acc[kh, rows, :] += dot(grad_half, q_blk, NN)
-        dqt[x_] += dot(turned[kh], grad_half, NN)
-        row_acc[x_, 0:1, :] += jnp.sum(grad, axis=0, keepdims=True)
-        if B > 64:
+        dqt[x_, :, part] += dot(turned[kh], grad_half, NN)
+        row_acc[x_, 0:1, part] += jnp.sum(grad, axis=0, keepdims=True)
+        if count >= 128:
             folded = grad[:, 0:128]
-            for lane in range(128, 2 * B, 128):
+            for lane in range(128, count, 128):
                 folded = folded + grad[:, lane:lane + 128]
             cs_acc[kh, rows, :] += folded
         else:
-            cs_acc[kh, rows, 0:2 * B] += grad
+            cs_acc[kh, rows, 0:count] += grad
 
     def key_turn(turned, rows):
         for kh in range(2):
@@ -377,10 +385,20 @@
         for arr in range(2):
             drain(q_block((q_all, g_all)[arr], x_, 1 - c), sib_r.at[arr, x_])
 
+    def piece_totals(row):
+        return jnp.sum(jnp.where(in_piece, jnp.broadcast_to(row, (8, B)), 0.0), axis=1, keepdims=True)
+
+    lane_at = iota((8, 128), 1)
+
+    def note(kind, row):
+        after_own[...] = jnp.where(lane_at == kind * Z + row_at, piece_totals(row), after_own[...])
+
     def curve_send(slot):
         rows, dy = pl.ds(slot * HB, HB), order[slot]
         column = jnp.concatenate([cs_acc[0, rows, :], cs_acc[1, rows, :]], axis=0)
-        cs_snd[slot] = jnp.broadcast_to(jnp.sum(column.T, axis=0, keepdims=True), (8, B))
+        sums = jnp.sum(column.T, axis=0, keepdims=True)
+        cs_snd[slot] = sums
+        note(X * CORES + (y + dy) % Y, sums)
         send(cs_snd.at[slot], cs_rcv.at[0, y], cs_s.at[0], cs_r.at[0], y_dev(dy), dy == 0)
         send(cs_snd.at[slot], cs_rcv.at[1, y], cs_s.at[1], cs_r.at[1], dev(xr, z, c, (y + dy) % Y), False)
 
@@ -415,18 +433,19 @@
             sib_wait((x + x_order[i]) % X)
 
     def rows_done(x_):
-        tiles = halves(row_acc[x_, :, 0:B], row_acc[x_, :, B:2 * B])
-        for c_ in range(CORES):
-            rs_snd[x_ * CORES + c_] = tiles[c_]
-            src, dst = rs_snd.at[x_ * CORES + c_], rs_rcv.at[xc]
-            here = jnp.logical_and(x_ == x, c_ == c)
-            send(src, dst, rs_s.at[0], rs_r.at[0], dev(x_, z, c_, y), here)
         dq_part = dqt[x_].T * scale
         for hf in range(2):
             lower, upper = dq_part[hf * B:hf * B + HB], dq_part[hf * B + HB:hf * B + B]
             dqt_own[x_, hf] = jnp.where(c == 0, lower, upper)
             sib_snd[x_, hf] = jnp.where(c == 0, upper, lower).astype(BF16)
         remote(sib_snd.at[x_], sib_rcv.at[x_], dsib_s.at[x_], dsib_r.at[x_], sibling).start()
+        tiles = halves(row_acc[x_, :, 0:B], row_acc[x_, :, B:2 * B])
+        for c_ in range(CORES):
+            rs_snd[x_ * CORES + c_] = tiles[c_][0:1]
+            note(x_ * CORES + c_, tiles[c_][0:1])
+            src, dst = rs_snd.at[x_ * CORES + c_], rs_rcv.at[xc]
+            here = jnp.logical_and(x_ == x, c_ == c)
+            send(src, dst, rs_s.at[0], rs_r.at[0], dev(x_, z, c_, y), here)
 
     def rows_home(x_):
         drain(sib_rcv.at[x_], dsib_r.at[x_])
@@ -455,19 +474,22 @@
             x_ = (x + pick(x_order, X - 1 - i if last else i)) % X
 
             def key_half(kh, inner):
-                first = jnp.where(kh == 0, x, xr)
-
-                @pl.when(x_ > first)
+                @pl.when(x_ > jnp.where(kh == 0, x, xr))
                 def _():
-                    pair(x_, kh, rows, turned, False)
-
-                @pl.when(x_ == first)
-                def _():
-                    pair(x_, kh, rows, turned, True)
+                    pair(x_, kh, rows, turned, 0, False)
 
                 return inner
 
             lax.fori_loop(0, 2, key_half, 0)
+
+            @pl.when(x_ == x)
+            def _():
+                pair(x_, 0, rows, turned, 0, True)
+
+            @pl.when(x_ == xr)
+            def _():
+                pair(x_, 1, rows, turned, B, True)
+
             if last:
                 rows_done(x_)
 
@@ -489,6 +511,9 @@
         band(first_slot, slots, kt_all[b], b == len(bands) - 1, None if b else query_steps)
         for slot in range(first_slot, first_slot + slots):
             curve_send(slot)
+        if b == len(bands) - 1:
+            after_all[x * CY + cy] = jnp.sum(after_own[...], axis=0, keepdims=True)
+            spread(after_all, x * CY + cy, t_r.at[1], t_s.at[1])
         if b:
             for slot in range(first_slot, first_slot + slots):
                 key_send(slot)
@@ -510,23 +535,6 @@
         dq_sum = dq_sum + dq_rcv[x_].astype(F32)
     dq_fin[...] = dq_sum.astype(BF16)
     give_back(dq_fin, dq_out, 0, False)
-
-    drain(rs_rcv, rs_r.at[0])
-    drain(cs_rcv.at[0], cs_r.at[0])
-    drain(cs_rcv.at[1], cs_r.at[1])
-    rows_sum = jnp.zeros((8, B), F32)
-    for x_ in range(X):
-        for c_ in range(CORES):
-            rows_sum = rows_sum + rs_rcv[x_ * CORES + c_]
-    columns_sum = jnp.zeros((8, B), F32)
-    for y_ in range(Y):
-        columns_sum = columns_sum + jnp.where(low, cs_rcv[0, y_], cs_rcv[1, y_])
-    later = section_scan(jnp.broadcast_to(rows_sum[0:1], (8, B)) - columns_sum, R, Z, True)
-    totals = jnp.zeros((8, 128), F32)
-    for s in range(Z):
-        totals = jnp.where(row_at == s, jnp.broadcast_to(later[0:1, s * R:s * R + 1], (8, 128)), totals)
-    after_all[x * CY + cy] = totals
-    spread(after_all, x * CY + cy, t_r.at[1], t_s.at[1])
 
     for rcv, acc, fin, out, idx, factor in (
         (dk_rcv, dk_acc, dk_fin, dk_out, 1, scale), (dv_rcv, dv_acc, dv_fin, dv_out, 2, 1.0)
@@ -539,27 +547,56 @@
             fin[kh] = sums[kh].astype(BF16)
         give_back(fin, out, idx, True)
 
+    drain(rs_rcv, rs_r.at[0])
+    drain(cs_rcv.at[0], cs_r.at[0])
+    drain(cs_rcv.at[1], cs_r.at[1])
+    rows_sum = jnp.zeros((1, B), F32)
+    for x_ in range(X):
+        for c_ in range(CORES):
+            rows_sum = rows_sum + rs_rcv[x_ * CORES + c_]
+    columns_sum = jnp.zeros((1, B), F32)
+    for y_ in range(Y):
+        columns_sum = columns_sum + jnp.where(low[0:1], cs_rcv[0, y_], cs_rcv[1, y_])
+    later = section_scan(jnp.broadcast_to(rows_sum - columns_sum, (8, B)), R, Z, True)
     drain(after_all.at[pl.ds(0, few)], t_r.at[1])
-    after = jnp.zeros((8, 128), F32)
-    for x_ in range(X):
-        level = jnp.zeros((8, 128), F32)
-        for k in range(CY):
-            tile = after_all[x_ * CY + k]
-            level = level + tile
-            after = after + jnp.where(jnp.logical_and(x_ == x, k > cy), tile, 0.0)
-        after = after + jnp.where(x_ == x, row_scan(level, True), 0.0)
-        after = after + jnp.where(x_ > x, jnp.sum(level, axis=0, keepdims=True), 0.0)
+    kind_at = section_of(lane_at, Z, X * CORES + Y)
+    piece_at = lane_at - Z * kind_at
+    of_x = section_of(kind_at, CORES, X + Y)
+    turn_at = (kind_at - CORES * of_x) * Y
+    later_x = own_x = own_later = jnp.zeros((8, 128), F32)
+    for y_ in range(Y):
+        tile = sum(after_all[(x_ * CORES + c_) * Y + y_] for x_ in range(X) for c_ in range(CORES))
+        tile = jnp.where(kind_at < X * CORES, tile, 0.0)
+        own = jnp.where(of_x == x, tile, 0.0)
+        later_x = later_x + jnp.where(of_x > x, tile, 0.0)
+        own_x = own_x + own
+        own_later = own_later + jnp.where(turn_at + y_ > cy, own, 0.0)
+    column_at = kind_at - X * CORES
+    is_column = jnp.logical_and(column_at >= 0, column_at < Y)
+    for c_ in range(CORES):
+        tiles = [
+            jnp.where(is_column, sum(after_all[(x_ * CORES + c_) * Y + y_] for y_ in range(Y)), 0.0)
+            for x_ in range(X)
+        ]
+        for x_ in range(X):
+            tile = jnp.where(piece_at < half, tiles[x_], tiles[X - 1 - x_])
+            own = jnp.where(x_ == x, tile, 0.0)
+            later_x = later_x - jnp.where(x_ > x, tile, 0.0)
+            own_x = own_x - own
+            own_later = own_later - jnp.where(column_at + c_ * Y > cy, own, 0.0)
+    terms = later_x + jnp.where(piece_at > row_at, own_x, 0.0) + jnp.where(piece_at == row_at, own_later, 0.0)
+    after = jnp.broadcast_to(jnp.sum(terms, axis=1, keepdims=True), (8, 128))
     gate_sum = later + along_lanes(after)
     for s in range(Z):
         moved = pltpu.roll(gate_sum, (B - s * R) % B, 1) if s else gate_sum
-        gs_snd[s] = moved[:, 0:128] if B >= 128 else jnp.concatenate([moved, jnp.zeros((8, 128 - B), F32)], axis=1)
+        gs_snd[s] = (moved[:, 0:128] if B >= 128 else jnp.concatenate([moved, jnp.zeros((8, 128 - B), F32)], axis=1))[0:1]
     for d in z_order:
         zz = (z + d) % Z
         send(gs_snd.at[zz], gs_rcv.at[z], f_s.at[3], f_r.at[3], dev(x, zz, c, y), d == 0)
     drain(gs_rcv, f_r.at[3])
     by_head = jnp.zeros((8, 128), F32)
     for h in range(H):
-        by_head = by_head + jnp.where(row_at == h, gs_rcv[h], 0.0)
+        by_head = by_head + jnp.where(row_at == h, jnp.broadcast_to(gs_rcv[h], (8, 128)), 0.0)
     dgate_out[...] = (by_head[0:H, 0:R] * jax.nn.sigmoid(-gate_float)).astype(BF16)
 
     for arr in range(2):
@@ -628,20 +665,20 @@
     block, tile = (2, HB, D), (8, 128)
     scratch = [
         vm((R, columns), BF16), vm((R, columns), BF16), vm(tile, F32),
-        vm((H,) + tile, F32), vm((Z,) + tile, F32), vm((Z,) + tile, F32),
-        vm(queries, BF16), vm(queries, BF16), vm((X * C, 8, B), F32),
-        vm(keys, BF16), vm(keys, BF16), vm((Y, 8, B), F32),
+        vm((H, 2, 128), F32), vm((H, 1, 128), F32), vm((Z, 2, 128), F32), vm((Z, 1, 128), F32),
+        vm(queries, BF16), vm(queries, BF16), vm((X * C, 2, B), F32),
+        vm(keys, BF16), vm(keys, BF16), vm((Y, 1, B), F32),
         vm((2, Y * HB, 128), F32), vm((Y * HB, 128), jnp.int32),
         vm((X * C * Y,) + tile, F32), vm((X * C * Y,) + tile, F32),
         vm((2, D, HB), BF16), vm((2, D, 2 * HB), BF16), vm((2, D, HB), BF16), vm((X, 8, 2 * B), F32),
         vm((X, D, 2 * B), F32), vm((X,) + block, F32), vm((X, 8, 2 * B), F32),
         vm(keys, F32), vm(keys, F32), vm((2, Y * HB, 128), F32),
         vm((X,) + block, BF16), vm((X,) + block, BF16), vm((X,) + block, BF16), vm((X,) + block, BF16),
-        vm((X * C, 8, B), F32), vm((X * C, 8, B), F32),
+        vm((X * C, 1, B), F32), vm((X * C, 1, B), F32),
         vm((Y,) + block, BF16), vm((Y,) + block, BF16), vm((Y,) + block, BF16), vm((Y,) + block, BF16),
-        vm((Y, 8, B), F32), vm((2, Y, 8, B), F32),
-        vm((X * C * Y,) + tile, F32), vm(block, BF16), vm(block, BF16), vm(block, BF16),
-        vm((Z,) + tile, F32), vm((H,) + tile, F32),
+        vm((Y, 1, B), F32), vm((2, Y, 1, B), F32),
+        vm(tile, F32), vm((X * C * Y, 1, 128), F32), vm(block, BF16), vm(block, BF16), vm(block, BF16),
+        vm((Z, 1, 128), F32), vm((H, 1, 128), F32),
         dma((2,)), dma((6,)), dma((6,)), dma((2, 3)), dma((2, 3)), dma((2, 3)), dma((2, 3)),
         dma((2, X)), dma((2, X)), dma((1,)), dma((1,)), dma((1,)), dma((1,)),
         dma((2,)), dma((2,)), dma((X,)), dma((X,)), dma((X,)), dma((X,)), dma((1,)), dma((1,)),

time: 65.3 us -> 62.3 us (0.954)
  Pallas kernels: 60.6 us -> 57.7 us
    pallas_call x1, Pallas kernels: 60.6 us -> 57.7 us  [per_device(): pl.pallas_call(functools.partial(body, X, Z, Y, R), out_shape=(big, big,...]
where the time goes in v4:
time: 62.3 us; the launch traced here: 62 us
  Pallas kernels  57.7 us (93%)
  local copies, waits for them, and re-layouts  3.74 us (6%)
  between operations  0.65 us (1%)
    pallas_call x1, Pallas kernels, per_device(): pl.pallas_call(functools.partial(body, X, Z, Y, R), out_shape=(big, big,...  57.7 us
    unnamed x10, local copies, waits for them, and re-layouts  3.74 us

profile of v4, /device:TPU:1, one launch (start us, length us, event | category | flops | bytes accessed | tf_op | source)
XLA Modules:
  0.0 62.0 jit_solution(8081603434850752967)
XLA Ops:
  0.6 57.7 %shard_map.102 = (bf16[48,1024]{1,0:T(8,128)(2,1)}, bf16[48,1024]{1,0:T(8,128)(2,1)}, bf16[48,1024]{1,0:T(8,128)(2,1)}, bf16[8,48]{1,0:T(8,128)(2,1)}) custom-call(bf16[48,1024]{1,0:T(8,128)(2,1)} %q_in.1, bf16[48,1024]{1,0:T(8,128)(2,1)} %k_in.1, bf16[48,1024]{1,0:T(8,128)(2,1)} %v_in.1, bf16[48,1024]{1,0:T(8,128)(2,1)} %g_in.1, bf16[48,1024]{1,0:T(8,128)(2,1)} %o_in.1, ...), custom_call_target="tpu_custom_call" | custom-call | tf_op jit(solution)/shard_map/pallas_call | solution.py:688
  58.3 0.0 copy-start.1
  58.3 1.6 %copy.15 = bf16[48,1024]{1,0:T(8,128)(2,1)} copy(bf16[48,1024]{1,0:T(8,128)(2,1)} %get-tuple-element.16) | data formatting | bytes 196608
  59.9 0.0 copy-done.1
  59.9 0.0 copy-start
  59.9 0.6 %copy.16 = bf16[48,1024]{1,0:T(8,128)(2,1)} copy(bf16[48,1024]{1,0:T(8,128)(2,1)S(1)} %copy-done.1) | data formatting | bytes 196608
  60.5 0.3 copy-done
  60.8 0.0 copy-start.2
  60.8 0.6 %copy.17 = bf16[48,1024]{1,0:T(8,128)(2,1)} copy(bf16[48,1024]{1,0:T(8,128)(2,1)S(1)} %copy-done) | data formatting | bytes 196608
  61.5 0.0 copy-done.2
  61.5 0.6 copy.18
Async XLA Ops:
  58.3 1.6 %copy-start.1 = (bf16[48,1024]{1,0:T(8,128)(2,1)S(1)}, bf16[48,1024]{1,0:T(8,128)(2,1)}, u32[]{:S(2)}) copy-start(bf16[48,1024]{1,0:T(8,128)(2,1)} %get-tuple-element.17) | copy-start | bytes 294916
  59.9 0.9 %copy-start = (bf16[48,1024]{1,0:T(8,128)(2,1)S(1)}, bf16[48,1024]{1,0:T(8,128)(2,1)}, u32[]{:S(2)}) copy-start(bf16[48,1024]{1,0:T(8,128)(2,1)} %get-tuple-element.18) | copy-start | bytes 294916
  60.8 0.7 %copy-start.2 = (bf16[8,48]{1,0:T(8,128)(2,1)S(1)}, bf16[8,48]{1,0:T(8,128)(2,1)}, u32[]{:S(2)}) copy-start(bf16[8,48]{1,0:T(8,128)(2,1)} %get-tuple-element.11) | copy-start | bytes 2308

commit v5 on v4

--- a/solution.py
+++ b/solution.py
@@ -65,7 +65,7 @@
     X, Z, Y, R,
     q_in, k_in, v_in, g_in, o_in, gate_in, lse_in,
     dq_out, dk_out, dv_out, dgate_out,
-    g_loc, o_loc, gate_pad, st_q, st_k, qst_in, kst_in,
+    g_loc, o_loc, gate_loc, lse_loc, gate_pad, st_q, st_k, qst_in, kst_in,
     q_all, g_all, qst_all, k_all, v_all, kst_all, kcol, kpos, tot_all, p_all,
     kt_own, kt_next, kt_far, q_row, dqt, dqt_own, row_acc, dk_acc, dv_acc, cs_acc,
     sib_snd, sib_rcv, dq_snd, dq_rcv, rs_snd, rs_rcv, dk_snd, dv_snd, dk_rcv, dv_rcv, cs_snd, cs_rcv,
@@ -115,6 +115,8 @@
     loc = [
         pltpu.make_async_copy(g_in, g_loc, loc_sem.at[0]),
         pltpu.make_async_copy(o_in, o_loc, loc_sem.at[1]),
+        pltpu.make_async_copy(gate_in, gate_loc, loc_sem.at[2]),
+        pltpu.make_async_copy(lse_in, lse_loc, loc_sem.at[3]),
     ]
     for copy in loc:
         copy.start()
@@ -136,10 +138,10 @@
     st_q[...] = jnp.zeros_like(st_q)
     st_k[...] = jnp.zeros_like(st_k)
     gate_pad[...] = jnp.zeros_like(gate_pad)
-    gate_float = gate_in[...].astype(F32)
+    gate_float = gate_loc[...].astype(F32)
     gate_pad[0:H, 0:R] = jax.nn.log_sigmoid(gate_float)
     curve = section_scan(gate_pad[...], R, 1, False)
-    lse_rows = lse_in[...]
+    lse_rows = lse_loc[...]
     for h in range(H):
         cut = slice(h * D, (h + 1) * D)
         product = g_loc[:, cut].astype(F32) * o_loc[:, cut].astype(F32)
@@ -439,6 +441,8 @@
             dqt_own[x_, hf] = jnp.where(c == 0, lower, upper)
             sib_snd[x_, hf] = jnp.where(c == 0, upper, lower).astype(BF16)
         remote(sib_snd.at[x_], sib_rcv.at[x_], dsib_s.at[x_], dsib_r.at[x_], sibling).start()
+
+    def rows_curve(x_):
         tiles = halves(row_acc[x_, :, 0:B], row_acc[x_, :, B:2 * B])
         for c_ in range(CORES):
             rs_snd[x_ * CORES + c_] = tiles[c_][0:1]
@@ -509,14 +513,16 @@
             for arr in range(2):
                 ring_last(keys, arr, k_id, Y, y_r)
         band(first_slot, slots, kt_all[b], b == len(bands) - 1, None if b else query_steps)
-        for slot in range(first_slot, first_slot + slots):
-            curve_send(slot)
-        if b == len(bands) - 1:
-            after_all[x * CY + cy] = jnp.sum(after_own[...], axis=0, keepdims=True)
-            spread(after_all, x * CY + cy, t_r.at[1], t_s.at[1])
         if b:
             for slot in range(first_slot, first_slot + slots):
                 key_send(slot)
+
+    for x_ in range(X):
+        rows_curve(x_)
+    for slot in range(Y):
+        curve_send(slot)
+    after_all[x * CY + cy] = jnp.sum(after_own[...], axis=0, keepdims=True)
+    spread(after_all, x * CY + cy, t_r.at[1], t_s.at[1])
 
     def give_back(fin, out, idx, keyed):
         for d in z_order:
@@ -664,7 +670,7 @@
     queries, keys = (X, 2, C * HB, D), (2, Y * HB, D)
     block, tile = (2, HB, D), (8, 128)
     scratch = [
-        vm((R, columns), BF16), vm((R, columns), BF16), vm(tile, F32),
+        vm((R, columns), BF16), vm((R, columns), BF16), vm((H, R), BF16), vm((H, R), F32), vm(tile, F32),
         vm((H, 2, 128), F32), vm((H, 1, 128), F32), vm((Z, 2, 128), F32), vm((Z, 1, 128), F32),
         vm(queries, BF16), vm(queries, BF16), vm((X * C, 2, B), F32),
         vm(keys, BF16), vm(keys, BF16), vm((Y, 1, B), F32),
@@ -679,7 +685,7 @@
         vm((Y, 1, B), F32), vm((2, Y, 1, B), F32),
         vm(tile, F32), vm((X * C * Y, 1, 128), F32), vm(block, BF16), vm(block, BF16), vm(block, BF16),
         vm((Z, 1, 128), F32), vm((H, 1, 128), F32),
-        dma((2,)), dma((6,)), dma((6,)), dma((2, 3)), dma((2, 3)), dma((2, 3)), dma((2, 3)),
+        dma((4,)), dma((6,)), dma((6,)), dma((2, 3)), dma((2, 3)), dma((2, 3)), dma((2, 3)),
         dma((2, X)), dma((2, X)), dma((1,)), dma((1,)), dma((1,)), dma((1,)),
         dma((2,)), dma((2,)), dma((X,)), dma((X,)), dma((X,)), dma((X,)), dma((1,)), dma((1,)),
         dma((2, Y)), dma((2, Y)), dma((2,)), dma((2,)), dma((4,)), dma((4,)),
@@ -688,7 +694,7 @@
     dq, dk, dv, dgate = pl.pallas_call(
         functools.partial(body, X, Z, Y, R),
         out_shape=(big, big, big, jax.ShapeDtypeStruct((H, R), BF16)),
-        in_specs=[any_spec] * 5 + [vm_spec] * 2,
+        in_specs=[any_spec] * 7,
         out_specs=(any_spec, any_spec, any_spec, vm_spec),
         scratch_shapes=scratch,
         compiler_params=pltpu.CompilerParams(

time: 62.3 us -> 59.7 us (0.958)
  Pallas kernels: 57.7 us -> 55.1 us
    pallas_call x1, Pallas kernels: 57.7 us -> 55.1 us  [per_device(): pl.pallas_call(functools.partial(body, X, Z, Y, R), out_shape=(big, big,...]
where the time goes in v5:
time: 59.7 us; the launch traced here: 59.5 us
  Pallas kernels  55.1 us (92%)
  local copies, waits for them, and re-layouts  3.74 us (6%)
  between operations  0.65 us (1%)
    pallas_call x1, Pallas kernels, per_device(): pl.pallas_call(functools.partial(body, X, Z, Y, R), out_shape=(big, big,...  55.1 us
    unnamed x10, local copies, waits for them, and re-layouts  3.74 us

profile of v5, /device:TPU:1, one launch (start us, length us, event | category | flops | bytes accessed | tf_op | source)
XLA Modules:
  0.0 59.5 jit_solution(752070909416936212)
XLA Ops:
  0.6 55.1 %shard_map.102 = (bf16[48,1024]{1,0:T(8,128)(2,1)}, bf16[48,1024]{1,0:T(8,128)(2,1)}, bf16[48,1024]{1,0:T(8,128)(2,1)}, bf16[8,48]{1,0:T(8,128)(2,1)}) custom-call(bf16[48,1024]{1,0:T(8,128)(2,1)} %q_in.1, bf16[48,1024]{1,0:T(8,128)(2,1)} %k_in.1, bf16[48,1024]{1,0:T(8,128)(2,1)} %v_in.1, bf16[48,1024]{1,0:T(8,128)(2,1)} %g_in.1, bf16[48,1024]{1,0:T(8,128)(2,1)} %o_in.1, ...), custom_call_target="tpu_custom_call" | custom-call | tf_op jit(solution)/shard_map/pallas_call | solution.py:694
  55.7 0.0 copy-start.1
  55.7 1.6 %copy.15 = bf16[48,1024]{1,0:T(8,128)(2,1)} copy(bf16[48,1024]{1,0:T(8,128)(2,1)} %get-tuple-element.16) | data formatting | bytes 196608
  57.3 0.0 copy-done.1
  57.3 0.0 copy-start
  57.3 0.6 %copy.16 = bf16[48,1024]{1,0:T(8,128)(2,1)} copy(bf16[48,1024]{1,0:T(8,128)(2,1)S(1)} %copy-done.1) | data formatting | bytes 196608
  58.0 0.3 copy-done
  58.2 0.0 copy-start.2
  58.2 0.6 %copy.17 = bf16[48,1024]{1,0:T(8,128)(2,1)} copy(bf16[48,1024]{1,0:T(8,128)(2,1)S(1)} %copy-done) | data formatting | bytes 196608
  58.9 0.0 copy-done.2
  58.9 0.6 copy.18
Async XLA Ops:
  55.7 1.6 %copy-start.1 = (bf16[48,1024]{1,0:T(8,128)(2,1)S(1)}, bf16[48,1024]{1,0:T(8,128)(2,1)}, u32[]{:S(2)}) copy-start(bf16[48,1024]{1,0:T(8,128)(2,1)} %get-tuple-element.17) | copy-start | bytes 294916
  57.3 0.9 %copy-start = (bf16[48,1024]{1,0:T(8,128)(2,1)S(1)}, bf16[48,1024]{1,0:T(8,128)(2,1)}, u32[]{:S(2)}) copy-start(bf16[48,1024]{1,0:T(8,128)(2,1)} %get-tuple-element.18) | copy-start | bytes 294916
  58.2 0.7 %copy-start.2 = (bf16[8,48]{1,0:T(8,128)(2,1)S(1)}, bf16[8,48]{1,0:T(8,128)(2,1)}, u32[]{:S(2)}) copy-start(bf16[8,48]{1,0:T(8,128)(2,1)} %get-tuple-element.11) | copy-start | bytes 2308

commit v6 on v5

--- a/solution.py
+++ b/solution.py
@@ -424,13 +424,13 @@
                 for arr in range(2):
                     ring_other(queries, arr, q_id, X, x_r)
                     to_sibling(arr, (x + 1) % X if arr == 0 else (x + X - 1) % X)
-        if i == X - 1:
-            for arr in range(2):
-                ring_onward(keys, arr, k_id, Y, y_dev, y_s, y_r)
         if i == 3:
             for arr in range(2):
                 ring_last(queries, arr, q_id, X, x_r)
                 to_sibling(arr, (x + 2) % X)
+        if i == X - 1:
+            for arr in range(2):
+                ring_onward(keys, arr, k_id, Y, y_dev, y_s, y_r)
         if i:
             sib_wait((x + x_order[i]) % X)
 
@@ -698,9 +698,9 @@
         out_specs=(any_spec, any_spec, any_spec, vm_spec),
         scratch_shapes=scratch,
         compiler_params=pltpu.CompilerParams(
-            collective_id=0, has_side_effects=True, vmem_limit_bytes=63 * 1024 * 1024
+            collective_id=0, has_side_effects=True, vmem_limit_bytes=48 * 1024 * 1024
         ),
-    )(*args[:5], args[5].T, args[6].T)
+    )(*(pltpu.with_memory_space_constraint(value, pltpu.HBM) for value in (*args[:5], args[5].T, args[6].T)))
     return dq, dk, dv, dgate.T
 
 

time: 59.7 us -> 57.3 us (0.960)
  local copies, waits for them, and re-layouts: 3.74 us -> 2.5 us
  Pallas kernels: 55.1 us -> 53.9 us
    unnamed x10 -> x4, local copies, waits for them, and re-layouts: 3.74 us -> 2.5 us
    pallas_call x1, Pallas kernels: 55.1 us -> 53.9 us  [per_device(): pl.pallas_call(functools.partial(body, X, Z, Y, R), out_shape=(big, big,...]
where the time goes in v6:
time: 57.3 us; the launch traced here: 57.1 us
  Pallas kernels  53.9 us (94%)
  local copies, waits for them, and re-layouts  2.5 us (4%)
  between operations  0.64 us (1%)
    pallas_call x1, Pallas kernels, per_device(): pl.pallas_call(functools.partial(body, X, Z, Y, R), out_shape=(big, big,...  53.9 us
    unnamed x4, local copies, waits for them, and re-layouts  2.5 us

profile of v6, /device:TPU:1, one launch (start us, length us, event | category | flops | bytes accessed | tf_op | source)
XLA Modules:
  0.0 57.1 jit_solution(5648217271335540425)
XLA Ops:
  0.6 53.9 %shard_map.102 = (bf16[48,1024]{1,0:T(8,128)(2,1)S(1)}, bf16[48,1024]{1,0:T(8,128)(2,1)S(1)}, bf16[48,1024]{1,0:T(8,128)(2,1)S(1)}, bf16[8,48]{1,0:T(8,128)(2,1)S(1)}) custom-call(bf16[48,1024]{1,0:T(8,128)(2,1)} %q_in.1, bf16[48,1024]{1,0:T(8,128)(2,1)} %k_in.1, bf16[48,1024]{1,0:T(8,128)(2,1)} %v_in.1, bf16[48,1024]{1,0:T(8,128)(2,1)} %g_in.1, ...), custom_call_target="tpu_custom_call" | custom-call | tf_op jit(solution)/shard_map/pallas_call | solution.py:694
  54.6 0.6 %copy.15 = bf16[48,1024]{1,0:T(8,128)(2,1)} copy(bf16[48,1024]{1,0:T(8,128)(2,1)S(1)} %get-tuple-element.16) | data formatting | bytes 196608
  55.2 0.6 %copy.16 = bf16[48,1024]{1,0:T(8,128)(2,1)} copy(bf16[48,1024]{1,0:T(8,128)(2,1)S(1)} %get-tuple-element.17) | data formatting | bytes 196608
  55.9 0.6 %copy.17 = bf16[48,1024]{1,0:T(8,128)(2,1)} copy(bf16[48,1024]{1,0:T(8,128)(2,1)S(1)} %get-tuple-element.18) | data formatting | bytes 196608
  56.5 0.6 %copy.18 = bf16[48,8]{0,1:T(8,128)(2,1)} copy(bf16[48,8]{0,1:T(8,128)(2,1)S(1)} %bitcast.3) | data formatting | bytes 1536

commit v7 on v6

--- a/solution.py
+++ b/solution.py
@@ -64,7 +64,7 @@
 def body(
     X, Z, Y, R,
     q_in, k_in, v_in, g_in, o_in, gate_in, lse_in,
-    dq_out, dk_out, dv_out, dgate_out,
+    grads_out, dgate_out,
     g_loc, o_loc, gate_loc, lse_loc, gate_pad, st_q, st_k, qst_in, kst_in,
     q_all, g_all, qst_all, k_all, v_all, kst_all, kcol, kpos, tot_all, p_all,
     kt_own, kt_next, kt_far, q_row, dqt, dqt_own, row_acc, dk_acc, dv_acc, cs_acc,
@@ -73,6 +73,7 @@
     loc_sem, p1_r, p1_s, x_r, x_s, y_r, y_s, sib_r, sib_s, qs_r, qs_s, ks_r, ks_s,
     t_r, t_s, dsib_r, dsib_s, dq_r, dq_s, rs_r, rs_s, dk_r, dk_s, cs_r, cs_s, f_r, f_s,
 ):
+    dq_out, dk_out, dv_out = (grads_out.at[k] for k in range(3))
     D, H = WIDTH, Z
     half, CY = Z // 2, CORES * Y
     HB, B = half * R, Z * R
@@ -690,18 +691,17 @@
         dma((2,)), dma((2,)), dma((X,)), dma((X,)), dma((X,)), dma((X,)), dma((1,)), dma((1,)),
         dma((2, Y)), dma((2, Y)), dma((2,)), dma((2,)), dma((4,)), dma((4,)),
     ]
-    big = jax.ShapeDtypeStruct((R, columns), BF16)
-    dq, dk, dv, dgate = pl.pallas_call(
+    grads, dgate = pl.pallas_call(
         functools.partial(body, X, Z, Y, R),
-        out_shape=(big, big, big, jax.ShapeDtypeStruct((H, R), BF16)),
+        out_shape=(jax.ShapeDtypeStruct((3, R, columns), BF16), jax.ShapeDtypeStruct((H, R), BF16)),
         in_specs=[any_spec] * 7,
-        out_specs=(any_spec, any_spec, any_spec, vm_spec),
+        out_specs=(any_spec, vm_spec),
         scratch_shapes=scratch,
         compiler_params=pltpu.CompilerParams(
             collective_id=0, has_side_effects=True, vmem_limit_bytes=48 * 1024 * 1024
         ),
     )(*(pltpu.with_memory_space_constraint(value, pltpu.HBM) for value in (*args[:5], args[5].T, args[6].T)))
-    return dq, dk, dv, dgate.T
+    return grads[0], grads[1], grads[2], dgate.T
 
 
 def solution(mesh):

time: 57.3 us -> 56.1 us (0.979)
  local copies, waits for them, and re-layouts: 2.5 us -> 1.29 us
    unnamed x4 -> x1, local copies, waits for them, and re-layouts: 2.5 us -> 0.58 us
    squeeze x0 -> x1, local copies, waits for them, and re-layouts: none -> 0.71 us  [per_device(): return (grads[0], grads[1], grads[2], dgate.T)]
where the time goes in v7:
time: 56.1 us; the launch traced here: 55.8 us
  Pallas kernels  53.9 us (96%)
  local copies, waits for them, and re-layouts  1.29 us (2%)
  between operations  0.64 us (1%)
    pallas_call x1, Pallas kernels, per_device(): pl.pallas_call(functools.partial(body, X, Z, Y, R), out_shape=(jax.ShapeD...  53.9 us

profile of v7, /device:TPU:1, one launch (start us, length us, event | category | flops | bytes accessed | tf_op | source)
XLA Modules:
  0.0 55.8 jit_solution(6986068483357063143)
XLA Ops:
  0.6 53.9 %shard_map.102 = (bf16[3,48,1024]{2,1,0:T(8,128)(2,1)S(1)}, bf16[8,48]{1,0:T(8,128)(2,1)S(1)}) custom-call(bf16[48,1024]{1,0:T(8,128)(2,1)} %q_in.1, bf16[48,1024]{1,0:T(8,128)(2,1)} %k_in.1, bf16[48,1024]{1,0:T(8,128)(2,1)} %v_in.1, bf16[48,1024]{1,0:T(8,128)(2,1)} %g_in.1, bf16[48,1024]{1,0:T(8,128)(2,1)} %o_in.1, bf16[8,48]{1,0:T(8,128)(2,1)} %bitcast.11, ...), custom_call_target="tpu_custom_call" | custom-call | tf_op jit(solution)/shard_map/pallas_call | solution.py:694
  54.5 0.7 %slice_bitcast_fusion = (bf16[48,1024]{1,0:T(8,128)(2,1)}, bf16[48,1024]{1,0:T(8,128)(2,1)}, bf16[48,1024]{1,0:T(8,128)(2,1)}) fusion(bf16[3,48,1024]{2,1,0:T(8,128)(2,1)S(1)} %get-tuple-element.6), kind=kLoop, calls=%fused_computation | loop fusion | bytes 589824 | tf_op jit(solution)/shard_map/squeeze | solution.py:704
  55.3 0.6 %copy.12 = bf16[48,8]{0,1:T(8,128)(2,1)} copy(bf16[48,8]{0,1:T(8,128)(2,1)S(1)} %bitcast.9) | data formatting | bytes 1536

commit v8 on v7

--- a/solution.py
+++ b/solution.py
@@ -303,6 +303,18 @@
     q_rest = q_rest - HB * q_c
     q_z = section_of(q_rest, R, half)
     qpos = (q_half * half + q_z) * (CY * R) + q_c * (Y * R) + y * R + (q_rest - R * q_z)
+
+    def key_start(arr):
+        drain(keys[arr](0), p1_r.at[2 + arr])
+        ring_start(keys, arr, k_id, Y, y_dev, y_s, y_r)
+
+    def query_onward(arr):
+        if X > 1:
+            ring_onward(queries, arr, q_id, X, x_dev, x_s, x_r)
+            to_sibling(arr, (x + X - 1) % X if arr == 0 else (x + 1) % X)
+
+    key_start(0)
+    query_onward(0)
 
     few = X * CY - 1
     drain(tot_all.at[pl.ds(0, few)], t_r.at[0])
@@ -418,9 +430,6 @@
 
     def query_steps(i):
         if i == 1:
-            for arr in range(2):
-                ring_onward(queries, arr, q_id, X, x_dev, x_s, x_r)
-                to_sibling(arr, (x + X - 1) % X if arr == 0 else (x + 1) % X)
             if X > 2:
                 for arr in range(2):
                     ring_other(queries, arr, q_id, X, x_r)
@@ -463,9 +472,8 @@
     def pick(values, at):
         return sum(jnp.where(at == k, v, 0) for k, v in enumerate(values))
 
-    for arr in range(2):
-        drain(keys[arr](0), p1_r.at[2 + arr])
-        ring_start(keys, arr, k_id, Y, y_dev, y_s, y_r)
+    key_start(1)
+    query_onward(1)
     sib_wait(x)
 
     def band(first_slot, slots, turned, last, before_step):

time: 56.1 us -> 56.5 us (level)
  no operation moved by 1% of the time
where the time goes in v8:
time: 56.5 us; the launch traced here: 56.4 us
  Pallas kernels  54.4 us (96%)
  local copies, waits for them, and re-layouts  1.29 us (2%)
  between operations  0.64 us (1%)
    pallas_call x1, Pallas kernels, per_device(): pl.pallas_call(functools.partial(body, X, Z, Y, R), out_shape=(jax.ShapeD...  54.4 us

profile of v8, /device:TPU:1, one launch (start us, length us, event | category | flops | bytes accessed | tf_op | source)
XLA Modules:
  0.0 56.4 jit_solution(7931825978737182797)
XLA Ops:
  0.6 54.4 %shard_map.102 = (bf16[3,48,1024]{2,1,0:T(8,128)(2,1)S(1)}, bf16[8,48]{1,0:T(8,128)(2,1)S(1)}) custom-call(bf16[48,1024]{1,0:T(8,128)(2,1)} %q_in.1, bf16[48,1024]{1,0:T(8,128)(2,1)} %k_in.1, bf16[48,1024]{1,0:T(8,128)(2,1)} %v_in.1, bf16[48,1024]{1,0:T(8,128)(2,1)} %g_in.1, bf16[48,1024]{1,0:T(8,128)(2,1)} %o_in.1, bf16[8,48]{1,0:T(8,128)(2,1)} %bitcast.11, ...), custom_call_target="tpu_custom_call" | custom-call | tf_op jit(solution)/shard_map/pallas_call | solution.py:702
  55.1 0.7 %slice_bitcast_fusion = (bf16[48,1024]{1,0:T(8,128)(2,1)}, bf16[48,1024]{1,0:T(8,128)(2,1)}, bf16[48,1024]{1,0:T(8,128)(2,1)}) fusion(bf16[3,48,1024]{2,1,0:T(8,128)(2,1)S(1)} %get-tuple-element.6), kind=kLoop, calls=%fused_computation | loop fusion | bytes 589824 | tf_op jit(solution)/shard_map/squeeze | solution.py:712
  55.8 0.6 %copy.12 = bf16[48,8]{0,1:T(8,128)(2,1)} copy(bf16[48,8]{0,1:T(8,128)(2,1)S(1)} %bitcast.9) | data formatting | bytes 1536
